TPU v7x, 32 devices: a whole 2x2x4 slice. The times are simulated.
32 devices in a mesh: dp: 8 (over z, x), tensor: 4 (over y, core).
Axes of the slice: x: 2, y: 2, z: 4, core: 2. Of those that a mesh axis runs over, the one named last changes fastest.
Arguments:
- block_input: float32 [18912, 768], P(('dp', 'tensor')), may hold values from -6 to 6
- cotangent: float32 [18912, 768], P(('dp', 'tensor')), may hold values from -6 to 6
- query_weight: float32 [768, 768], P('dp', 'tensor'), may hold values from -0.21875 to 0.21875
- key_weight: float32 [768, 768], P('dp', 'tensor'), may hold values from -0.21875 to 0.21875
- value_weight: float32 [768, 768], P('dp', 'tensor'), may hold values from -0.21875 to 0.21875
- output_weight: float32 [768, 768], P('tensor', 'dp'), may hold values from -1.75 to 1.75
- first_gain: float32 [768], P('dp'), may hold values from 0.5 to 1.5
- first_shift: float32 [768], P('dp'), may hold values from -1 to 1
- expert_in: float32 [8, 768, 3072], P(None, 'dp', 'tensor'), may hold values from -0.21875 to 0.21875
- expert_out: float32 [8, 3072, 768], P(None, 'tensor', 'dp'), may hold values from -0.21875 to 0.21875
- second_gain: float32 [768], P('dp'), may hold values from 0.5 to 1.5
- second_shift: float32 [768], P('dp'), may hold values from -1 to 1
- routes: int32 [18912, 2], P('dp'), may hold values from 0 to 7, all different within a row; in each aligned block of 2364 rows (0 to 2363, 2364 to 4727, ...) at most 792 rows name the same one
- route_gates: float32 [18912, 2], P('dp'), may hold values from 0.25 to 0.75
- clip_threshold: float32 [12], P('tensor'), may hold values from 3 to 9
Outputs:
- block_output: float32 [18912, 768], P(('dp', 'tensor'))
- input_grad: float32 [18912, 768], P(('dp', 'tensor'))
- query_grad: float32 [768, 768], P('dp', 'tensor')
- key_grad: float32 [768, 768], P('dp', 'tensor')
- value_grad: float32 [768, 768], P('dp', 'tensor')
- output_grad: float32 [768, 768], P('tensor', 'dp')
- first_gain_grad: float32 [768], P('dp')
- first_shift_grad: float32 [768], P('dp')
- expert_in_grad: float32 [8, 768, 3072], P(None, 'dp', 'tensor')
- expert_out_grad: float32 [8, 3072, 768], P(None, 'tensor', 'dp')
- second_gain_grad: float32 [768], P('dp')
- second_shift_grad: float32 [768], P('dp')
- clipped_query: float32 [768, 768], P('dp', 'tensor')
- clipped_key: float32 [768, 768], P('dp', 'tensor')
- head_maxima: float32 [12], P('tensor')
Inputs may be any that keep to these rules, and one draw needn't show every extreme that they name: `routes`: each row names two different experts. In each aligned block of 2364 rows (the tokens of one index of dp) no expert is named by more than 792 rows, a bound that some block reaches.
All inputs are finite; a program needn't handle non-finite values.
Results may differ from a plain program's by a relative error of at most 0.018.
Values may be sent and summed in bfloat16 or wider, within the bound.
No kernel may reach another device: no remote copies, remote signals or barrier semaphores. Data moves between devices by JAX's collectives and lax.ppermute only.
A program may use at most 320 MiB of HBM per device.

v0:
```python
import functools
import math

import jax
import jax.numpy as jnp
from jax import lax
from jax.experimental import pallas as pl
from jax.experimental.pallas import tpu as pltpu
from jax.sharding import PartitionSpec as P

HD = 64
SEQ = 197
CAP = 792
EPSILON = 1e-06
F32 = jnp.float32
BF16 = jnp.bfloat16
OUTER = 8
EXTRA = 16
ROW_TILE = 256
WINDOW = 256
MIB = 1 << 20


def up(number, unit):
    return -(-number // unit) * unit


def dot(left, right, contract=((1,), (0,))):
    return lax.dot_general(left, right, (contract, ((), ())), preferred_element_type=F32)


def params(mib):
    return pltpu.CompilerParams(vmem_limit_bytes=mib * MIB)


def any_spec():
    return pl.BlockSpec(memory_space=pl.ANY)


def vmem_spec():
    return pl.BlockSpec(memory_space=pltpu.VMEM)


def smem_spec():
    return pl.BlockSpec(memory_space=pltpu.SMEM)


def sds(shape, dtype):
    return jax.ShapeDtypeStruct(shape, dtype)


def cost(microseconds):
    return pl.CostEstimate(flops=int(microseconds * 0.5e9), bytes_accessed=0, transcendentals=0)


def after(value, *others):
    return lax.optimization_barrier((value, *others))[0]


def block_flip(x_bit, low_bit, high_bit):
    return x_bit | low_bit << 1 | high_bit << 2


def norm_stats(values):
    mean = jnp.mean(values, -1, keepdims=True)
    centred = values - mean
    scale = lax.rsqrt(jnp.mean(centred * centred, -1, keepdims=True) + EPSILON)
    return centred * scale, scale


def spread_rows(source, target, images, stride):
    for i in range(images):
        target[i * stride : i * stride + SEQ, :] = source[i * SEQ : (i + 1) * SEQ, :].astype(F32)
        end = (i + 1) * stride if i + 1 < images else target.shape[0]
        target[i * stride + SEQ : end, :] = jnp.zeros((end - i * stride - SEQ, target.shape[1]), F32)


def gather_rows(source, target, images, stride):
    for i in range(images):
        target[i * SEQ : (i + 1) * SEQ, :] = source[i * stride : i * stride + SEQ, :]


def attention_forward_kernel(images, stride, heads, layout, *refs):
    n_pieces = len(layout)
    place_ref, x_ref, gains_ref = refs[:3]
    piece_refs = refs[3 : 3 + n_pieces]
    res_ref, second_ref, first_ref, w_ref, kept_ref, peak_ref = refs[3 + n_pieces : 9 + n_pieces]
    scratch, sems = refs[9 + n_pieces :]
    columns = heads * HD
    block = w_ref.shape[1] // OUTER
    place = place_ref[0]
    copies = []
    for ref, entries in zip(piece_refs, layout):
        for j, (t, flip) in enumerate(entries):
            row = pl.multiple_of((place ^ flip) * block, 16)
            copies.append(
                pltpu.make_async_copy(
                    ref.at[j, pl.ds(0, block), :],
                    w_ref.at[t, pl.ds(row, block), :],
                    sems.at[len(copies)],
                )
            )
            copies[-1].start()
    spread_rows(x_ref, res_ref, images, stride)
    unit, _ = norm_stats(res_ref[...])
    first_ref[...] = (unit * gains_ref[0:1, :] + gains_ref[1:2, :]).astype(BF16)
    for copy in copies:
        copy.wait()
    scale = 1.0 / math.sqrt(HD)
    key_ok = lax.broadcasted_iota(jnp.int32, (stride, stride), 0) < SEQ
    query_ok = lax.broadcasted_iota(jnp.int32, (1, stride), 1) < SEQ
    lane = lax.broadcasted_iota(jnp.int32, (8, 128), 1)

    def step(t, carry):
        scratch[...] = dot(first_ref[...], w_ref[t]).astype(BF16).astype(F32)
        peaks = jnp.full((8, 128), -jnp.inf, F32)
        for i in range(images):
            rows = slice(i * stride, (i + 1) * stride)
            for h in range(heads):
                at = [slice((1 + p) * columns + h * HD, (1 + p) * columns + (h + 1) * HD) for p in range(3)]
                q = (scratch[rows, at[0]] * scale).astype(BF16)
                k = scratch[rows, at[1]].astype(BF16)
                v = scratch[rows, at[2]].astype(BF16)
                s = jnp.where(key_ok, dot(k, q, ((1,), (1,))), -1e30)
                top = jnp.max(s, 0, keepdims=True)
                e = jnp.exp(s - top)
                p = e * (1.0 / jnp.sum(e, 0, keepdims=True))
                o = dot(v, p.astype(BF16), ((0,), (0,))).T
                scratch[rows, h * HD : (h + 1) * HD] = o.astype(BF16).astype(F32)
                peak = jnp.max(jnp.where(query_ok, top, -jnp.inf), keepdims=True)
                peaks = jnp.maximum(peaks, jnp.where(lane == h, peak, -jnp.inf))
        peak_ref[t] = peaks
        kept_ref[t] = scratch[...].astype(BF16)
        res_ref[...] += dot(kept_ref[t, :, 0:columns], w_ref[t, :, 0:columns], ((1,), (1,)))
        return carry

    lax.fori_loop(0, w_ref.shape[0], step, 0)
    unit, _ = norm_stats(res_ref[...])
    second_ref[...] = (unit * gains_ref[2:3, :] + gains_ref[3:4, :]).astype(BF16)


def attention_forward(place, rows, gains, pieces, layout, images, stride, padded, parts, heads):
    features = rows.shape[1]
    n_copies = sum(len(entries) for entries in layout)
    return pl.pallas_call(
        functools.partial(attention_forward_kernel, images, stride, heads, layout),
        out_shape=(
            sds((padded, features), F32),
            sds((padded, features), BF16),
            sds((padded, features), BF16),
            sds((parts, features, features), BF16),
            sds((parts, padded, features), BF16),
            sds((parts, 8, 128), F32),
        ),
        in_specs=[smem_spec(), vmem_spec(), vmem_spec()] + [any_spec()] * len(pieces),
        out_specs=(vmem_spec(),) * 6,
        scratch_shapes=[
            pltpu.VMEM((padded, features), F32),
            pltpu.SemaphoreType.DMA((n_copies,)),
        ],
        compiler_params=params(48),
        cost_estimate=cost(22),
        name="attention_forward",
    )(place, rows, gains, *pieces)


def head_at(columns, part, head):
    return slice(part * columns + head * HD, part * columns + (head + 1) * HD)


def norm_back(grad, gain, unit, scale):
    weighted = grad * gain
    mean = jnp.mean(weighted, -1, keepdims=True)
    return (weighted - mean - unit * jnp.mean(weighted * unit, -1, keepdims=True)) * scale


def heads_backward(images, stride, heads, t, w_ref, kept_ref, half_ref, firsts, halves, kept, mixed, grads, total):
    columns = heads * HD
    features = w_ref.shape[2]
    scale = 1.0 / math.sqrt(HD)
    key_ok = lax.broadcasted_iota(jnp.int32, (stride, stride), 0) < SEQ
    kept[...] = kept_ref[t, 0].astype(F32)
    mixed[...] = dot(half_ref[...], w_ref[t, 0, :, 0:columns]).astype(BF16).astype(F32)
    for i in range(images):
        rows = slice(i * stride, (i + 1) * stride)
        for h in range(heads):
            q = (kept[rows, head_at(columns, 1, h)] * scale).astype(BF16)
            k = kept[rows, head_at(columns, 2, h)].astype(BF16)
            v = kept[rows, head_at(columns, 3, h)].astype(BF16)
            do = mixed[rows, h * HD : (h + 1) * HD].astype(BF16)
            s = jnp.where(key_ok, dot(k, q, ((1,), (1,))), -1e30)
            e = jnp.exp(s - jnp.max(s, 0, keepdims=True))
            p = e * (1.0 / jnp.sum(e, 0, keepdims=True))
            dp = dot(v, do, ((1,), (1,)))
            dv = dot(p.astype(BF16), do)
            ds = (p * (dp - jnp.sum(p * dp, 0, keepdims=True))).astype(BF16)
            dq = dot(k, ds, ((0,), (0,))).T * scale
            dk = dot(ds, q)
            grads[rows, head_at(columns, 1, h)] = dq
            grads[rows, head_at(columns, 2, h)] = dk
            grads[rows, head_at(columns, 3, h)] = dv
    packed = grads[...].astype(BF16)
    total[...] += dot(packed, w_ref[t, 0], ((1,), (1,)))
    full = dot(firsts[...], packed)
    out = dot(halves[...], kept_ref[t, 0, :, 0:columns])
    full = full + jnp.concatenate((out, jnp.zeros((features, features - columns), F32)), 1)
    return full.astype(BF16)


def half_spec(value, y):
    return pl.BlockSpec((2, 1) + value.shape[2:], lambda i: (0, y, 0, 0))


def put_blocks(refs, t, full):
    block = full.shape[0] // OUTER
    for i, ref in enumerate(refs):

        @pl.when(t == i)
        def _(ref=ref):
            for j in range(OUTER):
                ref[j, 0:block, :] = full[j * block : (j + 1) * block, :]


def attention_backward_kernel(images, stride, heads, *refs):
    (cot_ref, res_ref, d0_ref, d1_ref, d2_ref, first_ref, w_ref, kept_ref, gains_ref, extra_ref) = refs[:10]
    keep_ref, send_ref, resid, half, total, firsts, halves, more_ref = refs[10:18]
    kept, grads, mixed = refs[18:]
    features = w_ref.shape[2]
    unit, scale_two = norm_stats(res_ref[...])
    da2 = d0_ref[...].astype(F32) + d1_ref[...].astype(F32) + d2_ref[...].astype(F32)
    row = lax.broadcasted_iota(jnp.int32, (EXTRA, features), 0)
    extra = jnp.where(row == 2, jnp.sum(da2 * unit, 0, keepdims=True), extra_ref[...])
    more_ref[...] = jnp.where(row == 3, jnp.sum(da2, 0, keepdims=True), extra)
    spread_rows(cot_ref, resid, images, stride)
    resid[...] += norm_back(da2, gains_ref[2:3, :], unit, scale_two)
    half[...] = resid[...].astype(BF16)
    firsts[...] = first_ref[...].T
    halves[...] = half[...].T
    total[...] = jnp.zeros_like(total)
    grads[...] = jnp.zeros_like(grads)

    def step(t, carry):
        full = heads_backward(
            images, stride, heads, t, w_ref, kept_ref, half, firsts, halves, kept, mixed, grads, total
        )
        put_blocks((keep_ref, send_ref), t, full)
        return carry

    lax.fori_loop(0, 2, step, 0)


def attention_rest_kernel(images, stride, heads, *refs):
    (x_ref, resid_ref, half, total_ref, firsts, halves, w_ref, kept_ref, gains_ref, more_ref) = refs[:10]
    input_grad_ref, keep_ref, send_ref, extra_ref = refs[10:14]
    kept, grads, mixed, total = refs[14:]
    features = w_ref.shape[2]
    block = features // OUTER
    total[...] = total_ref[...]
    grads[...] = jnp.zeros_like(grads)

    def step(t, carry):
        full = heads_backward(
            images, stride, heads, t, w_ref, kept_ref, half, firsts, halves, kept, mixed, grads, total
        )
        put_blocks((keep_ref, send_ref), t, full)
        return carry

    lax.fori_loop(0, 2, step, 0)
    spread_rows(x_ref, kept, images, stride)
    unit, scale_one = norm_stats(kept[...])
    da = total[...]
    grads[...] = resid_ref[...] + norm_back(da, gains_ref[0:1, :], unit, scale_one)
    gather_rows(grads, input_grad_ref, images, stride)
    row = lax.broadcasted_iota(jnp.int32, (EXTRA, features), 0)
    extra = jnp.where(row == 0, jnp.sum(da * unit, 0, keepdims=True), more_ref[...])
    extra = jnp.where(row == 1, jnp.sum(da, 0, keepdims=True), extra).astype(BF16)
    extra_ref[...] = extra
    for ref in (keep_ref, send_ref):
        for j in range(OUTER):
            ref[j, block : block + EXTRA, :] = extra


def attention_backward(cot, residual, pieces, first, weights, kept, gains, extra, images, stride, heads):
    padded, features = first.shape
    share = sds((OUTER, features // OUTER, features), BF16)
    wide, half, turned = sds((padded, features), F32), sds((padded, features), BF16), sds((features, padded), BF16)
    return pl.pallas_call(
        functools.partial(attention_backward_kernel, images, stride, heads),
        grid=(1,),
        out_shape=(share, share, wide, half, wide, turned, turned, sds((EXTRA, features), F32)),
        in_specs=[vmem_spec()] * 6 + [half_spec(weights, 1), half_spec(kept, 1)] + [vmem_spec()] * 2,
        out_specs=(vmem_spec(),) * 8,
        scratch_shapes=[
            pltpu.VMEM((padded, features), F32),
            pltpu.VMEM((padded, features), F32),
            pltpu.VMEM((padded, heads * HD), F32),
        ],
        compiler_params=params(50),
        cost_estimate=cost(20),
        name="attention_backward",
    )(cot, residual, *pieces, first, weights, kept, gains, extra)


def attention_rest(rows, resid, half, total, firsts, halves, weights, kept, gains, more, images, stride, heads):
    padded, features = resid.shape
    share = sds((OUTER, features // OUTER + EXTRA, features), BF16)
    return pl.pallas_call(
        functools.partial(attention_rest_kernel, images, stride, heads),
        grid=(1,),
        out_shape=(sds(rows.shape, F32), share, share, sds((EXTRA, features), BF16)),
        in_specs=[vmem_spec()] * 6 + [half_spec(weights, 0), half_spec(kept, 0)] + [vmem_spec()] * 2,
        out_specs=(vmem_spec(),) * 4,
        scratch_shapes=[
            pltpu.VMEM((padded, features), F32),
            pltpu.VMEM((padded, features), F32),
            pltpu.VMEM((padded, heads * HD), F32),
            pltpu.VMEM((padded, features), F32),
        ],
        compiler_params=params(50),
        cost_estimate=cost(20),
        name="attention_backward_rest",
    )(rows, resid, half, total, firsts, halves, weights, kept, gains, more)


def dispatch_kernel(gated, *refs):
    table_ref = refs[0]
    slot_ref = refs[-3] if gated else refs[-2]
    gate_ref = refs[-2] if gated else None
    out_ref = refs[-1]
    shard_refs = []
    for ref in refs[1 : -3 if gated else -2]:
        shard_refs += [ref] if len(ref.shape) == 2 else [ref.at[i] for i in range(ref.shape[0])]
    n_shards = len(shard_refs)
    expert = pl.program_id(0)
    experts = pl.num_programs(0)
    padded = shard_refs[0].shape[0]
    features = shard_refs[0].shape[1]
    count_all = table_ref[2 * n_shards * experts + expert]
    tail = pl.multiple_of(count_all // 16 * 16, 16)
    out_ref[0, pl.ds(tail, ROW_TILE + 16), :] = jnp.zeros((ROW_TILE + 16, features), BF16)
    row16 = lax.broadcasted_iota(jnp.int32, (16, 1), 0)
    rows = lax.broadcasted_iota(jnp.int32, (WINDOW, padded), 0)
    starts = [table_ref[expert * n_shards + r] for r in range(n_shards)]
    numbers = [table_ref[n_shards * experts + expert * n_shards + r] for r in range(n_shards)]
    firsts = [start // 16 * 16 for start in starts]
    steps = [
        (start - first + number + WINDOW - 1) // WINDOW
        for start, first, number in zip(starts, firsts, numbers)
    ]

    def step(r, c):
        low = pl.multiple_of(firsts[r] + c * WINDOW, 16)
        hit = slot_ref[0, r : r + 1, :] - low == rows
        chosen = jnp.where(hit, 1.0, 0.0)
        got = dot(chosen.astype(BF16), shard_refs[r][...])
        if gated:
            got = got * jnp.sum(chosen * gate_ref[0, r : r + 1, :], -1, keepdims=True)
        got = got.astype(BF16)
        before = out_ref[0, pl.ds(low, 16), :]
        out_ref[0, pl.ds(low, 16), :] = jnp.where(row16 + low < starts[r], before, got[:16])
        out_ref[0, pl.ds(low + 16, WINDOW - 16), :] = got[16:]

    short = functools.reduce(jnp.maximum, steps) <= 1

    @pl.when(short)
    def _():
        for r in range(n_shards):
            step(r, 0)

    @pl.when(jnp.logical_not(short))
    def _():
        for r in range(n_shards):

            def again(c, carry, r=r):
                step(r, c)
                return carry

            lax.fori_loop(0, steps[r], again, 0)


def slot_rows(limit):
    return up(limit, ROW_TILE) + WINDOW + 16


def dispatch(table, shards, slots, gates, limit):
    experts = slots.shape[0]
    padded, features = shards[0].shape[-2:]
    length = slot_rows(limit)
    gated = gates is not None
    per_expert = pl.BlockSpec((1,) + slots.shape[1:], lambda e: (e, 0, 0))
    return pl.pallas_call(
        functools.partial(dispatch_kernel, gated),
        grid=(experts,),
        out_shape=sds((experts, length, features), BF16),
        in_specs=[smem_spec()] + [vmem_spec()] * len(shards) + [per_expert] * (2 if gated else 1),
        out_specs=pl.BlockSpec((1, length, features), lambda e: (e, 0, 0)),
        compiler_params=params(48),
        cost_estimate=cost(15),
        name="dispatch_gated" if gated else "dispatch",
    )(table, *shards, slots, *([gates] if gated else []))


def normal_share(u):
    bell = jnp.exp(-0.5 * u * u)
    t = 1.0 / (1.0 + jnp.abs(u) * (0.3275911 / math.sqrt(2.0)))
    poly = 0.5 * 1.061405429
    for term in (-1.453152027, 1.421413741, -0.284496736, 0.254829592):
        poly = poly * t + 0.5 * term
    tail = poly * t * bell
    return jnp.where(u < 0, tail, 1.0 - tail), bell


def expert_kernel(*refs):
    info_ref, x_ref, dy_ref = refs[:3]
    w_refs = refs[3:11]
    y_ref, dx_ref = refs[11:13]
    share_refs = (refs[13:15], refs[15:17])
    w_in, w_out, g_in, g_out, hidden, slopes = refs[17:]
    place = info_ref[0]
    count = info_ref[1 + pl.program_id(0)]
    features = w_in.shape[0]
    block = features // OUTER
    for number, ref in enumerate(w_refs):
        flip = block_flip(number >> 2, number & 1, number >> 1 & 1)
        row = pl.multiple_of((place ^ flip) * block, 16)
        w_in[pl.ds(row, block), :] = ref[0, 0]
        w_out[pl.ds(row, block), :] = ref[0, 1]
    g_in[...] = jnp.zeros_like(g_in)
    g_out[...] = jnp.zeros_like(g_out)
    tiles = jnp.maximum((count + ROW_TILE - 1) // ROW_TILE, 1)

    def at(i):
        return pl.ds(pl.multiple_of(i * ROW_TILE, ROW_TILE), ROW_TILE)

    def first_half(i):
        pre = dot(x_ref[0, at(i), :], w_in[...])
        dh = dot(dy_ref[0, at(i), :], w_out[...])
        share, bell = normal_share(pre)
        hidden[i % 2] = (pre * share).astype(BF16)
        slope = share + pre * bell * (1.0 / math.sqrt(2.0 * math.pi))
        slopes[i % 2] = (dh * slope).astype(BF16)

    def second_half(i):
        hid, dpre = hidden[i % 2], slopes[i % 2]
        y_ref[0, at(i), :] = dot(hid, w_out[...], ((1,), (1,))).astype(BF16)
        dx_ref[0, at(i), :] = dot(dpre, w_in[...], ((1,), (1,))).astype(BF16)
        g_in[...] += dot(x_ref[0, at(i), :], dpre, ((0,), (0,)))
        g_out[...] += dot(dy_ref[0, at(i), :], hid, ((0,), (0,)))

    def tile(i, carry):
        second_half(i - 1)
        first_half(i)
        return carry

    first_half(0)
    lax.fori_loop(1, tiles, tile, 0)
    second_half(tiles - 1)
    rest = pl.ds(pl.multiple_of(tiles * ROW_TILE, 16), WINDOW + 16)
    y_ref[0, rest, :] = jnp.zeros((WINDOW + 16, features), BF16)
    dx_ref[0, rest, :] = jnp.zeros((WINDOW + 16, features), BF16)
    for number in range(OUTER):
        flip = block_flip(number >> 2 & 1, number & 1, number >> 1 & 1)
        row = pl.multiple_of((place ^ flip) * block, 16)
        in_ref, out_ref = share_refs[number // (OUTER // 2)]
        at = slice(number % (OUTER // 2) * block, (number % (OUTER // 2) + 1) * block)
        in_ref[0, at, :] = g_in[pl.ds(row, block), :].astype(BF16)
        out_ref[0, at, :] = g_out[pl.ds(row, block), :].astype(BF16)


def expert_math(info, x, dy, weights, first, experts, limit):
    length, features = x.shape[1:]
    hidden = weights[0].shape[3]
    most = up(limit, ROW_TILE)
    slots_spec = pl.BlockSpec((1, most, features), lambda e: (e + first, 0, 0))
    out_spec = pl.BlockSpec((1, length, features), lambda e: (e, 0, 0))
    share = sds((experts, features // 2, hidden), BF16)
    share_spec = pl.BlockSpec((1, features // 2, hidden), lambda e: (e, 0, 0))
    return pl.pallas_call(
        expert_kernel,
        grid=(experts,),
        out_shape=(sds((experts, length, features), BF16),) * 2 + (share,) * 4,
        in_specs=[smem_spec(), slots_spec, slots_spec]
        + [pl.BlockSpec((1,) + w.shape[1:], lambda e, at=first * (w.shape[0] > experts): (e + at, 0, 0, 0))
            for w in weights
],
        out_specs=(out_spec, out_spec) + (share_spec,) * 4,
        scratch_shapes=[
            pltpu.VMEM((features, hidden), BF16),
            pltpu.VMEM((features, hidden), BF16),
            pltpu.VMEM((features, hidden), F32),
            pltpu.VMEM((features, hidden), F32),
            pltpu.VMEM((2, ROW_TILE, hidden), BF16),
            pltpu.VMEM((2, ROW_TILE, hidden), BF16),
        ],
        compiler_params=params(60),
        cost_estimate=cost(33),
        name="expert_math",
    )(info, x, dy, *weights)


def combine_kernel(gated, n_sources, *refs):
    table_ref = refs[0]
    source_refs = refs[1 : 1 + n_sources]
    slot_ref = refs[1 + n_sources]
    gate_ref = refs[2 + n_sources] if gated else None
    send_ref, keep_ref, window = refs[-3:]
    r = pl.program_id(0)
    n_shards = pl.num_programs(0)
    per_source = source_refs[0].shape[0]
    experts = per_source * n_sources
    shard = lax.rem(r + n_shards // 2, n_shards)
    padded = slot_ref.shape[1]
    lanes = lax.broadcasted_iota(jnp.int32, (padded, WINDOW), 1)

    def chosen(e, low):
        hit = slot_ref[0, :, e : e + 1] == lanes + low
        return jnp.where(hit, gate_ref[0, :, e : e + 1] if gated else 1.0, 0.0).astype(BF16)

    firsts, steps, parts = [], [], []
    for e in range(experts):
        start = table_ref[e * n_shards + shard]
        number = table_ref[n_shards * experts + e * n_shards + shard]
        first = pl.multiple_of(start // 16 * 16, 16)
        firsts.append(first)
        steps.append((start - first + number + WINDOW - 1) // WINDOW)
        window[e * WINDOW : (e + 1) * WINDOW, :] = source_refs[e // per_source][e % per_source, pl.ds(first, WINDOW), :]
        parts.append(chosen(e, first))
    total = dot(jnp.concatenate(parts, 1), window[...]).astype(BF16)

    def finish(ref):
        ref[0] = total
        for e in range(experts):

            def step(c, carry, e=e):
                low = pl.multiple_of(firsts[e] + c * WINDOW, 16)
                rows = source_refs[e // per_source][e % per_source, pl.ds(low, WINDOW), :]
                ref[0] = (ref[0].astype(F32) + dot(chosen(e, low), rows)).astype(BF16)
                return carry

            lax.fori_loop(1, steps[e], step, 0)

    @pl.when(r < n_shards // 2)
    def _():
        finish(send_ref)

    @pl.when(r >= n_shards // 2)
    def _():
        finish(keep_ref)


def combine(table, sources, slots, gates):
    n_shards, padded, experts = slots.shape
    features = sources[0].shape[2]
    gated = gates is not None
    half = n_shards // 2
    per_shard = pl.BlockSpec((1, padded, experts), lambda r: (lax.rem(r + half, n_shards), 0, 0))
    share = sds((half, padded, features), BF16)
    return pl.pallas_call(
        functools.partial(combine_kernel, gated, len(sources)),
        grid=(n_shards,),
        out_shape=(share, share),
        in_specs=[smem_spec()] + [vmem_spec()] * len(sources) + [per_shard] * (2 if gated else 1),
        out_specs=(
            pl.BlockSpec((1, padded, features), lambda r: (jnp.minimum(r, half - 1), 0, 0)),
            pl.BlockSpec((1, padded, features), lambda r: (jnp.maximum(r - half, 0), 0, 0)),
        ),
        scratch_shapes=[pltpu.VMEM((experts * WINDOW, features), BF16)],
        compiler_params=params(48),
        cost_estimate=cost(2),
        name="combine_gated" if gated else "combine",
    )(table, *sources, slots, *([gates] if gated else []))


def spread_kernel(images, stride, x_ref, out_ref, scratch):
    spread_rows(x_ref, scratch, images, stride)
    out_ref[...] = scratch[...].astype(BF16)


def spread(rows, images, stride, padded):
    return pl.pallas_call(
        functools.partial(spread_kernel, images, stride),
        out_shape=sds((padded, rows.shape[1]), BF16),
        in_specs=[vmem_spec()],
        out_specs=vmem_spec(),
        scratch_shapes=[pltpu.VMEM((padded, rows.shape[1]), F32)],
        compiler_params=params(16),
        cost_estimate=cost(2),
        name="spread_rows",
    )(rows)


def finish_kernel(images, stride, res_ref, a_ref, b_ref, c_ref, out_ref, scratch):
    mixture = a_ref[...].astype(F32) + b_ref[...].astype(F32) + c_ref[...].astype(F32)
    scratch[...] = res_ref[...] + mixture
    gather_rows(scratch, out_ref, images, stride)


def finish(residual, pieces, tokens, images, stride):
    return pl.pallas_call(
        functools.partial(finish_kernel, images, stride),
        out_shape=sds((tokens, residual.shape[1]), F32),
        in_specs=[vmem_spec()] * 4,
        out_specs=vmem_spec(),
        scratch_shapes=[pltpu.VMEM(residual.shape, F32)],
        compiler_params=params(24),
        cost_estimate=cost(2),
        name="finish_rows",
    )(residual, *pieces)


def body(
    sizes,
    block_input,
    cotangent,
    query_weight,
    key_weight,
    value_weight,
    output_weight,
    first_gain,
    first_shift,
    expert_in,
    expert_out,
    second_gain,
    second_shift,
    routes,
    route_gates,
    clip_threshold,
):
    dp, tensor = sizes["dp"], sizes["tensor"]
    inner = dp // OUTER
    tokens, features = block_input.shape
    columns = query_weight.shape[1]
    heads = columns // HD
    images = tokens // SEQ
    stride = up(SEQ, 8)
    padded = up(images * stride, 16)
    experts = expert_in.shape[0]
    mine = experts // 2
    half = mine // 2
    block = features // OUTER
    limit = 2 * CAP
    dp_at = lax.axis_index("dp")
    place = dp_at // inner
    tensor_at = lax.axis_index("tensor")
    low_bit = place >> 1 & 1

    def along(axis, size, flip):
        pairs = [(i, i ^ flip) for i in range(size)]
        return lambda value: lax.ppermute(value, axis, pairs)

    send_x = along("dp", dp, 1 * inner)
    send_low = along("dp", dp, 2 * inner)
    send_high = along("dp", dp, 4 * inner)
    send_core = along("tensor", tensor, 1)
    send_y = along("tensor", tensor, 2)

    def whole_block(value, axis):
        if inner == 1:
            return value
        every = lax.all_gather(value, "dp", axis=axis, tiled=True)
        return lax.dynamic_slice_in_dim(every, place * block, block, axis)

    def own_rows(value, axis):
        if inner == 1:
            return value
        shape = list(value.shape)
        shape[axis] = features
        every = lax.dynamic_update_slice_in_dim(jnp.zeros(shape, value.dtype), value, place * block, axis)
        return lax.psum_scatter(every, "dp", scatter_dimension=axis, tiled=True)

    packed = jnp.concatenate(
        (output_weight.T, query_weight, key_weight, value_weight), 1
    ).astype(BF16)
    packed = whole_block(packed, 0)
    norms = jnp.stack((first_gain, first_shift, second_gain, second_shift)).astype(BF16)
    norms = whole_block(norms, 1)
    norms = lax.dynamic_update_slice(jnp.zeros((EXTRA, features), BF16), norms, (0, place * block))
    own = jnp.concatenate((packed, norms), 0)[None]
    cot_half = spread(cotangent, images, stride, padded)
    cot_y = send_y(cot_half)
    pair = jnp.concatenate((own, send_high(own)), 0)
    four = jnp.concatenate((pair, send_low(pair)), 0)
    four_x, four_y = send_x(four), send_y(four)
    cot_low = send_low(after(cot_half, four))

    w_in = whole_block(expert_in.astype(BF16), 1)
    w_out = whole_block(expert_out.astype(BF16), 2).swapaxes(1, 2)
    both = jnp.stack((w_in, w_out), 1)
    w_keep = lax.dynamic_slice_in_dim(both, low_bit * mine, mine, 0)
    w_give = lax.dynamic_slice_in_dim(both, (1 - low_bit) * mine, mine, 0)
    w_high_first = send_high(after(w_keep[:1], four))
    w_high_rest = send_high(after(w_keep[1:3], w_high_first))

    eight = jnp.concatenate((four, four_x), 0)
    two_a, two_b = send_x(after(four_y[:2], w_high_first)), send_y(four_x[2:])
    eight_y = after(jnp.concatenate((four_y, two_a, two_b), 0), cot_low)
    pieces = [eight, eight_y, send_core(eight), send_core(eight_y)]
    flips = tuple(block_flip(x_bit, low, high) for x_bit in (0, 1) for low in (0, 1) for high in (0, 1))
    layout = [tuple((t, flip) for flip in flips) for t in range(4)]
    gains = jnp.sum(eight[:, block:].astype(F32), 0)
    w_low = send_low(after(w_give, cot_low))
    cot_far = send_y(cot_low)
    w_keep_x = send_x(after(w_keep, two_a))

    table = jnp.concatenate((routes.T.astype(F32), route_gates.T), 0)
    picks = routes.shape[1]
    table = table.reshape(2 * picks, tensor, images, SEQ)
    table = jnp.pad(table, ((0, 0), (0, 0), (0, 0), (0, stride - SEQ)), constant_values=-1)
    table = table.reshape(2 * picks, tensor, images * stride)
    table = jnp.pad(table, ((0, 0), (0, 0), (0, padded - images * stride)), constant_values=-1)
    table = jnp.stack((table, send_low(table)))
    table = table.reshape(2, 2 * picks, 2, 2, padded)
    table = jnp.where(tensor_at >> 1 & 1 == 1, table[:, :, ::-1], table)
    table = jnp.where(tensor_at & 1 == 1, table[:, :, :, ::-1], table)
    table = table.transpose(1, 3, 0, 2, 4).reshape(2 * picks, 8, padded)
    ids = (low_bit * mine + jnp.arange(mine)).astype(F32)[None, :, None, None]
    hits = table[:picks, None] == ids
    chosen = jnp.any(hits, 0)
    gates = jnp.sum(jnp.where(hits, table[picks:, None], 0.0), 0)
    order = lax.broadcasted_iota(jnp.int32, (padded, padded), 0) < lax.broadcasted_iota(
        jnp.int32, (padded, padded), 1
    )
    before = jnp.dot(
        chosen.reshape(-1, padded).astype(BF16), order.astype(BF16), preferred_element_type=F32
    ).reshape(chosen.shape)
    counts = jnp.sum(chosen.astype(F32), -1)
    ahead = (jnp.arange(8)[:, None] < jnp.arange(8)[None, :]).astype(F32)
    starts = jnp.sum(counts[:, :, None] * ahead[None], 1)
    slots = jnp.where(chosen, starts[:, :, None] + before, -1.0).astype(jnp.int32)
    totals = jnp.sum(counts, 1)
    scalars = jnp.concatenate((starts.reshape(-1), counts.reshape(-1), totals)).astype(jnp.int32)
    slot_columns = slots.transpose(1, 2, 0)
    gate_columns = gates.transpose(1, 2, 0)

    place_word = place.astype(jnp.int32).reshape(1)
    residual, second, first, weights, kept, peaks = attention_forward(
        after(place_word, scalars, slots, gates, slot_columns, gate_columns), block_input, gains, pieces, layout, images, stride, padded, tensor, heads
    )
    second, w_low, w_high_rest, w_keep_x, cot_far = lax.optimization_barrier(
        (second, w_low, w_high_rest, w_keep_x, cot_far)
    )
    w_high_last = send_high(after(w_keep[3:], w_high_rest))

    by_low, by_y = send_low(second), send_y(second)
    w_low_x = send_x(w_low)
    cot_shards = jnp.stack((cot_half, cot_y, cot_low, cot_far))
    cot_slots = dispatch(scalars, (cot_shards, send_core(cot_shards)), slots, gates, limit)
    w_low_0 = send_high(after(w_low[:half], second))
    cot_slots, by_low, by_y, w_low_x, w_high_last = lax.optimization_barrier(
        (cot_slots, by_low, by_y, w_low_x, w_high_last)
    )
    w_high = jnp.concatenate((w_high_first, w_high_rest, w_high_last), 0)
    by_far = send_y(by_low)
    shards = [second, by_y, by_low, by_far]
    shards += [send_core(piece) for piece in shards]
    w_high_x = send_x(after(w_high, w_low_x))
    w_low_1 = send_high(after(w_low[half:], by_low))
    w_low_x_0 = send_x(after(w_low_0, w_high_x))
    x_slots = dispatch(after(scalars, w_low_0), shards, slots, None, limit)
    w_low_1 = after(w_low_1, x_slots)
    w_low_x_1 = send_x(w_low_1)

    def run_experts(c, x, weights):
        info = jnp.concatenate((place_word, totals[c * half : (c + 1) * half].astype(jnp.int32)))
        return expert_math(info, x, cot_slots, weights, c * half, half, limit)

    basic = (w_keep, w_low, w_high)
    basic_x = (w_keep_x, w_low_x, w_high_x)
    y_0, dx_0, *shares_0 = run_experts(0, after(x_slots, w_low_1), (*basic, w_low_0, *basic_x, w_low_x_0))
    keep_0, give_0 = shares_0[:2], shares_0[2:]
    give_0[0], x_slots = lax.optimization_barrier((give_0[0], x_slots, w_low_x_1))[:2]
    side_in_0 = send_x(give_0[0])
    y_1, dx_1, *shares_1 = run_experts(1, x_slots, (*basic, w_low_1, *basic_x, w_low_x_1))
    keep_1, give_1 = shares_1[:2], shares_1[2:]
    dx_1 = after(dx_1, side_in_0)
    side_out_0 = send_x(after(give_0[1], dx_1))
    rows = keep_0[0].shape[1] // 2

    def upper_sum(keep, side):
        return keep[:, rows:] + side[:, rows:]

    def lower_sum(keep, side, high):
        return (keep[:, :rows].astype(F32) + side[:, :rows].astype(F32) + high.astype(F32)).astype(BF16)

    high_in_0 = send_high(after(upper_sum(keep_0[0], side_in_0), dx_1))
    give, hold = combine(scalars, (dx_0, dx_1), slot_columns, None)
    give, side_out_0, high_in_0 = lax.optimization_barrier((give, side_out_0, high_in_0))
    core = send_core(give)
    high_out_0 = send_high(after(upper_sum(keep_0[1], side_out_0), give))
    sums = [hold[i] + core[i] for i in range(4)]
    far_y, near_y = send_y(sums[3]), send_y(sums[1])
    side_in_1 = send_x(after(give_1[0], give))
    give, hold_y = combine(after(scalars, sums[3]), (y_0, y_1), slot_columns, gate_columns)
    give, side_in_1, far_y, high_out_0 = lax.optimization_barrier((give, side_in_1, far_y, high_out_0))
    core_y = send_core(give)
    low = send_low(sums[2] + far_y)
    side_out_1 = send_x(after(give_1[1], give))
    mixture = [hold_y[i] + core_y[i] for i in range(4)]
    mixture_y = send_y(jnp.stack((mixture[1], mixture[3])))
    high_in_1 = send_high(after(upper_sum(keep_1[0], side_in_1), high_out_0))
    high_out_1 = send_high(after(upper_sum(keep_1[1], side_out_1), high_out_0))
    grad_pieces = (after(sums[0], *mixture), near_y, low)
    mine_0 = jnp.stack(
        (lower_sum(keep_0[0], side_in_0, high_in_0), lower_sum(keep_0[1], side_out_0, high_out_0)), 1
    )
    low_0 = send_low(mine_0[:, :, block:])

    peak = peaks[:, 0, :heads].reshape(2, 2, heads)
    peak = jnp.where(tensor_at & 1 == 1, peak[::-1], peak)
    peak = jnp.where(tensor_at >> 1 & 1 == 1, peak[:, ::-1], peak)
    peak = peak.transpose(1, 0, 2).reshape(tensor * heads)
    extra = jnp.zeros((EXTRA, features), F32)
    if inner == 1:
        device = dp_at * tensor + tensor_at
        high = lax.reduce_precision(peak, 8, 7)
        rest = lax.reduce_precision(peak - high, 8, 7)
        is_mine = (jnp.arange(dp * tensor) == device)[None, :, None]
        words = jnp.where(is_mine, jnp.stack((high, rest))[:, None, :], 0.0).reshape(2, -1)
        extra = extra.at[4:6, : words.shape[1]].set(words)
    weights = weights.reshape(2, 2, features, features)
    kept = kept.reshape(2, 2, padded, features)
    keep_b, send_b, resid, dattn, total, firsts, halves, extra = attention_backward(
        cotangent, residual, grad_pieces, first, weights, kept, gains, extra, images, stride, heads
    )
    total, send_b, mixture_y, high_in_1, low_0, side_out_1 = lax.optimization_barrier(
        (total, send_b, mixture_y, high_in_1, low_0, side_out_1)
    )
    upper = send_y(keep_b + send_core(send_b))
    mixture_low = send_low(mixture[2] + mixture_y[1])
    input_grad, keep, send, extra = attention_rest(
        block_input, resid, dattn, total, firsts, halves, weights, kept, gains, extra, images, stride, heads
    )
    send, extra, upper, high_out_1, mixture_low = lax.optimization_barrier(
        (send, extra, upper, high_out_1, mixture_low)
    )
    mine_1 = jnp.stack(
        (lower_sum(keep_1[0], side_in_1, high_in_1), lower_sum(keep_1[1], side_out_1, high_out_1)), 1
    )
    low_1 = send_low(mine_1[:, :, block:])

    near = send_core(send)
    extra_y = send_y(extra)
    extra_far = lax.ppermute(extra, "tensor", [(i, i ^ 3) for i in range(tensor)])
    others = jnp.broadcast_to(extra_y.astype(F32) + extra_far.astype(F32), (OUTER, EXTRA, features))
    others = jnp.concatenate((upper.astype(F32), others), 1)
    total = (keep.astype(F32) + near.astype(F32) + others).astype(BF16)
    total, low_1 = lax.optimization_barrier((total, low_1))
    block_output = finish(residual, (mixture[0], mixture_y[0], mixture_low), tokens, images, stride)

    own_share = jnp.concatenate((mine_0[:, :, :block], mine_1[:, :, :block]), 0)
    far_share = jnp.concatenate((low_0, low_1), 0)
    grads = jnp.concatenate(
        (
            jnp.where(low_bit == 0, own_share, far_share),
            jnp.where(low_bit == 0, far_share, own_share),
        ),
        0,
    ).astype(F32)
    expert_in_grad = own_rows(grads[:, 0], 1)
    expert_out_grad = own_rows(grads[:, 1].swapaxes(1, 2), 2)

    if inner == 1:
        total = lax.all_to_all(total, "dp", 0, 0, tiled=True)
        total = jnp.sum(total.astype(F32), 0)
        words = total[block:]
        total = total[:block]
        peak = jnp.sum(words[4:6, : dp * tensor * tensor * heads], 0).reshape(dp * tensor, tensor * heads)
        peak = jnp.max(peak, 0)
    else:
        words = lax.psum(total[0, block:].astype(F32), "dp")
        total = total[:, :block].reshape(features, features).astype(F32)
        total = lax.psum_scatter(total, "dp", scatter_dimension=0, tiled=True)
        peak = lax.pmax(peak, ("dp", "tensor"))
    head_maxima = lax.dynamic_slice_in_dim(peak, tensor_at * heads, heads, 0)
    vectors = lax.dynamic_slice_in_dim(words[:4], dp_at * (features // dp), features // dp, 1)
    output_grad, query_grad, key_grad, value_grad = (
        total[:, i * columns : (i + 1) * columns] for i in range(4)
    )
    factor = jnp.minimum(1.0, clip_threshold / jnp.maximum(head_maxima, 1.0))
    column_scale = jnp.repeat(jnp.sqrt(factor), HD)
    return (
        block_output,
        input_grad,
        query_grad,
        key_grad,
        value_grad,
        output_grad.T,
        vectors[0],
        vectors[1],
        expert_in_grad,
        expert_out_grad,
        vectors[2],
        vectors[3],
        query_weight * column_scale[None, :],
        key_weight * column_scale[None, :],
        head_maxima,
    )


def solution(mesh):
    rows = P(("dp", "tensor"), None)
    by_column, by_row, by_dp = P("dp", "tensor"), P("tensor", "dp"), P("dp")
    up_spec, down_spec = P(None, "dp", "tensor"), P(None, "tensor", "dp")
    sizes = dict(mesh.shape)
    return jax.shard_map(
        functools.partial(body, sizes),
        mesh=mesh,
        in_specs=(
            rows, rows, by_column, by_column, by_column, by_row, by_dp, by_dp, up_spec, down_spec,
            by_dp, by_dp, P("dp", None), P("dp", None), P("tensor"),
        ),
        out_specs=(
            rows, rows, by_column, by_column, by_column, by_row, by_dp, by_dp, up_spec, down_spec,
            by_dp, by_dp, by_column, by_column, P("tensor"),
        ),
        check_vma=False,
    )
```

profile of v0, /device:TPU:0, one launch (start us, length us, event | category | flops | bytes accessed | tf_op | source)
XLA Modules:
  0.0 510.9 jit_solution(2483977753658817364)
XLA Ops:
  2.4 3.1 collective-permute-start
  25.3 8.1 %collective-permute-done.2 = bf16[2,112,768]{2,1,0:T(8,128)(2,1)S(1)} collective-permute-done((bf16[2,112,768]{2,1,0:T(8,128)(2,1)S(1)}, bf16[2,112,768]{2,1,0:T(8,128)(2,1)S(1)}, u32[]{:S(2)}, u32[]{:S(2)}) %collective-permute-start.2) | collective-permute-done | bytes 344096 | tf_op jit(solution)/shard_map/ppermute | solution.py:649
  42.6 9.6 %collective-permute-done.3 = bf16[4,112,768]{2,1,0:T(8,128)(2,1)S(1)} collective-permute-done((bf16[4,112,768]{2,1,0:T(8,128)(2,1)}, bf16[4,112,768]{2,1,0:T(8,128)(2,1)S(1)}, u32[]{:S(2)}, u32[]{:S(2)}) %collective-permute-start.3) | collective-permute-done | bytes 688160 | tf_op jit(solution)/shard_map/ppermute | solution.py:649
  61.6 4.1 collective-permute-done.6
  82.6 22.1 %attention_forward.1 = (f32[608,768]{1,0:T(8,128)}, bf16[608,768]{1,0:T(8,128)(2,1)S(1)}, bf16[608,768]{1,0:T(8,128)(2,1)S(1)}, bf16[4,768,768]{2,1,0:T(8,128)(2...) custom-call(s32[1]{0:T(128)} %bitcast.refs_0_, f32[591,768]{1,0:T(8,128)} %refs_0_.3, ...), custom_call_target="tpu_custom_call" | custom-call | flops 11000000512 | tf_op jit(solution)/shard_map/attention_forward/pallas_call | solution.py:145
  105.6 8.6 %collective-permute-done.12 = bf16[2,2,96,768]{3,2,1,0:T(8,128)(2,1)S(1)} collective-permute-done((bf16[2,2,96,768]{3,2,1,0:T(8,128)(2,1)}, bf16[2,2,96,768]{3,2,1,0:T(8,128)(2,1)S(1)}, u32[]{:S(2)}, u32[]{:S(2)}) %collective-permute-start.12) | collective-permute-done | bytes 589856 | tf_op jit(solution)/shard_map/ppermute | solution.py:649
  122.0 2.9 collective-permute-done.17.refs_2_
  124.9 17.3 %dispatch_gated.1.refs_2_ = bf16[4,2064,768]{2,1,0:T(8,128)(2,1)} custom-call(s32[68]{0:T(128)S(1)} %copy-done.3, bf16[4,608,768]{2,1,0:T(8,128)(2,1)S(1)} %pad_maximum_fusion.refs_1_, bf16[4,608,768]{2,1,0:T(8,128)(2,1)} %collective-permute-done.17.refs_2_, s32[4,8,608]{2,1,0:T(8,128)S(1)} %copy-done.2, f32[4,8,608]{2,1,0:T(8,128)S(1)} %fusion.22.refs_4_), custom_call_target="tpu_custom_call" | custom-call | flops 7500000256 | tf_op jit(solution)/shard_map/dispatch_gated/pallas_call | solution.py:391
  142.2 4.5 collective-permute-done.21
  154.4 23.2 %collective-permute-done.15.refs_6_ = bf16[2,2,96,768]{3,2,1,0:T(8,128)(2,1)S(1)} collective-permute-done((bf16[2,2,96,768]{3,2,1,0:T(8,128)(2,1)S(1)}, bf16[2,2,96,768]{3,2,1,0:T(8,128)(2,1)S(1)}, u32[]{:S(2)}, u32[]{:S(2)}) %collective-permute-start.15) | collective-permute-done | bytes 589856 | tf_op jit(solution)/shard_map/ppermute | solution.py:649
  183.0 15.5 %dispatch.1.refs_1_ = bf16[4,2064,768]{2,1,0:T(8,128)(2,1)} custom-call(s32[68]{0:T(128)S(1)} %copy-done.3, bf16[608,768]{1,0:T(8,128)(2,1)S(1)} %get-tuple-element.130.refs_1_, bf16[608,768]{1,0:T(8,128)(2,1)S(1)} %collective-permute-done.19.refs_2_, bf16[608,768]{1,0:T(8,128)(2,1)S(1)} %collective-permute-done.18.refs_3_, ...), custom_call_target="tpu_custom_call" | custom-call | flops 7500000256 | tf_op jit(solution)/shard_map/dispatch/pallas_call | solution.py:391
  198.6 9.3 %collective-permute-done.27.refs_6_ = bf16[2,2,96,768]{3,2,1,0:T(8,128)(2,1)} collective-permute-done((bf16[2,2,96,768]{3,2,1,0:T(8,128)(2,1)S(1)}, bf16[2,2,96,768]{3,2,1,0:T(8,128)(2,1)}, u32[]{:S(2)}, u32[]{:S(2)}) %collective-permute-start.27) | collective-permute-done | bytes 589856 | tf_op jit(solution)/shard_map/ppermute | solution.py:649
  208.9 33.7 %expert_math.2 = (bf16[2,2064,768]{2,1,0:T(8,128)(2,1)}, bf16[2,2064,768]{2,1,0:T(8,128)(2,1)}, bf16[2,384,768]{2,1,0:T(8,128)(2,1)}, bf16[2,384,768]{2,1,0:T(8,...) custom-call(s32[3]{0:T(128)} %pad_add_fusion.refs_0_, bf16[4,2064,768]{2,1,0:T(8,128)(2,1)} %dispatch.1.refs_1_, ...), custom_call_target="tpu_custom_call" | custom-call | flops 16499999744 | tf_op jit(solution)/shard_map/expert_math/pallas_call | solution.py:478
  243.7 34.0 %expert_math.3 = (bf16[2,2064,768]{2,1,0:T(8,128)(2,1)}, bf16[2,2064,768]{2,1,0:T(8,128)(2,1)}, bf16[2,384,768]{2,1,0:T(8,128)(2,1)}, bf16[2,384,768]{2,1,0:T(8,...) custom-call(s32[3]{0:T(128)} %pad_add_fusion.1.refs_0_, bf16[4,2064,768]{2,1,0:T(8,128)(2,1)} %dispatch.1.refs_1_, ...), custom_call_target="tpu_custom_call" | custom-call | flops 16499999744 | tf_op jit(solution)/shard_map/expert_math/pallas_call | solution.py:478
  281.7 17.9 %combine.1 = (bf16[4,608,768]{2,1,0:T(8,128)(2,1)}, bf16[4,608,768]{2,1,0:T(8,128)(2,1)}) custom-call(s32[68]{0:T(128)S(1)} %copy-done.3, bf16[2,2064,768]{2,1,0:T(8,128)(2,1)} %get-tuple-element.147.refs_1_, bf16[2,2064,768]{2,1,0:T(8,128)(2,1)} %get-tuple-element.152.refs_2_, s32[8,608,4]{2,1,0:T(8,128)S(1)} %fusion.2.refs_3_), custom_call_target="tpu_custom_call" | custom-call | flops 1000000000 | tf_op jit(solution)/shard_map/combine/pallas_call | solution.py:558
  299.6 2.8 collective-permute-done.33
  302.4 3.0 collective-permute-done.32
  306.5 5.6 %collective-permute-done.34 = bf16[4,608,768]{2,1,0:T(8,128)(2,1)S(1)} collective-permute-done((bf16[4,608,768]{2,1,0:T(8,128)(2,1)}, bf16[4,608,768]{2,1,0:T(8,128)(2,1)S(1)}, u32[]{:S(2)}, u32[]{:S(2)}) %collective-permute-start.34) | collective-permute-done | bytes 3735584 | tf_op jit(solution)/shard_map/ppermute | solution.py:649
  312.2 4.4 fusion.11
  320.0 19.4 %combine_gated.1 = (bf16[4,608,768]{2,1,0:T(8,128)(2,1)}, bf16[4,608,768]{2,1,0:T(8,128)(2,1)}) custom-call(s32[68]{0:T(128)S(1)} %copy-done.3, bf16[2,2064,768]{2,1,0:T(8,128)(2,1)} %get-tuple-element.161.refs_1_, bf16[2,2064,768]{2,1,0:T(8,128)(2,1)} %get-tuple-element.162.refs_2_, s32[8,608,4]{2,1,0:T(8,128)S(1)} %fusion.2.refs_3_, f32[8,608,4]{2,1,0:T(8,128)S(1)} %bitcast.92), custom_call_target="tpu_custom_call" | custom-call | flops 1000000000 | tf_op jit(solution)/shard_map/combine_gated/pallas_call | solution.py:558
  339.4 4.5 collective-permute-done.37
  361.6 8.2 %collective-permute-done.39.refs_3_ = bf16[608,768]{1,0:T(8,128)(2,1)S(1)} collective-permute-done((bf16[608,768]{1,0:T(8,128)(2,1)}, bf16[608,768]{1,0:T(8,128)(2,1)S(1)}, u32[]{:S(2)}, u32[]{:S(2)}) %collective-permute-start.39) | collective-permute-done | bytes 933920 | tf_op jit(solution)/shard_map/ppermute | solution.py:649
  369.8 11.5 %collective-permute-done.40.refs_4_ = bf16[608,768]{1,0:T(8,128)(2,1)S(1)} collective-permute-done((bf16[608,768]{1,0:T(8,128)(2,1)S(1)}, bf16[608,768]{1,0:T(8,128)(2,1)S(1)}, u32[]{:S(2)}, u32[]{:S(2)}) %collective-permute-start.40) | collective-permute-done | bytes 933920 | tf_op jit(solution)/shard_map/ppermute | solution.py:649
  381.3 21.4 %attention_backward.1 = (bf16[8,96,768]{2,1,0:T(8,128)(2,1)}, bf16[8,96,768]{2,1,0:T(8,128)(2,1)}, f32[608,768]{1,0:T(8,128)}, bf16[608,768]{1,0:T(8,128)(2,1)S(...) custom-call(f32[591,768]{1,0:T(8,128)} %refs_0_.2, ...), custom_call_target="tpu_custom_call" | custom-call | flops 10000000000 | tf_op jit(solution)/shard_map/attention_backward/pallas_call | solution.py:287
  402.8 6.8 %collective-permute-done.41 = bf16[2,608,768]{2,1,0:T(8,128)(2,1)} collective-permute-done((bf16[2,608,768]{2,1,0:T(8,128)(2,1)S(1)}, bf16[2,608,768]{2,1,0:T(8,128)(2,1)}, u32[]{:S(2)}, u32[]{:S(2)}) %collective-permute-start.41) | collective-permute-done | bytes 1867808 | tf_op jit(solution)/shard_map/ppermute | solution.py:649
  409.7 2.9 collective-permute-done.45
  415.1 19.6 %attention_backward_rest.1 = (f32[591,768]{1,0:T(8,128)}, bf16[8,112,768]{2,1,0:T(8,128)(2,1)}, bf16[8,112,768]{2,1,0:T(8,128)(2,1)}, bf16[16,768]{1,0:T(8,128)(2,1)S(1)}) custom-call(f32[591,768]{1,0:T(8,128)} %refs_0_.3, f32[608,768]{1,0:T(8,128)} %get-tuple-element.187.refs_1_, bf16[608,768]{1,0:T(8,128)(2,1)S(1)} %get-tuple-element.188.refs_2_, ...), custom_call_target="tpu_custom_call" | custom-call | flops 10000000000 | tf_op jit(solution)/shard_map/attention_backward_rest/pallas_call | solution.py:307
  434.7 4.5 collective-permute-done.47
  439.2 10.8 %collective-permute-done.48.c_ref = bf16[608,768]{1,0:T(8,128)(2,1)S(1)} collective-permute-done((bf16[608,768]{1,0:T(8,128)(2,1)S(1)}, bf16[608,768]{1,0:T(8,128)(2,1)S(1)}, u32[]{:S(2)}, u32[]{:S(2)}) %collective-permute-start.48) | collective-permute-done | bytes 933920 | tf_op jit(solution)/shard_map/ppermute | solution.py:649
  460.2 8.8 %collective-permute-done.52 = bf16[2,2,96,768]{3,2,0,1:T(8,128)(2,1)} collective-permute-done((bf16[2,2,96,768]{3,2,0,1:T(8,128)(2,1)S(1)}, bf16[2,2,96,768]{3,2,0,1:T(8,128)(2,1)}, u32[]{:S(2)}, u32[]{:S(2)}) %collective-permute-start.52) | collective-permute-done | bytes 589856 | tf_op jit(solution)/shard_map/ppermute | solution.py:649
  469.0 5.1 all-to-all-start
  483.5 23.3 %all-to-all-done = bf16[8,112,768]{2,1,0:T(8,128)(2,1)S(1)} async-done(((bf16[8,112,768]{2,1,0:T(8,128)(2,1)}), bf16[8,112,768]{2,1,0:T(8,128)(2,1)S(1)}, u32[]{:S(2)}, u32[]{:S(2)}) %all-to-all-start) | async-done | bytes 1376288 | tf_op jit(solution)/shard_map/all_to_all | solution.py:863
  (310 shorter events, 132.8 us)
Async XLA Ops:
  2.4 38.0 %collective-permute-start = (f32[4,4,608]{2,1,0:T(4,128)S(1)}, f32[4,4,608]{2,1,0:T(4,128)S(1)}, u32[]{:S(2)}, u32[]{:S(2)}) collective-permute-start(f32[4,4,608]{2,1,0:T(4,128)S(1)} %pad.14), channel_id=1, source_target_pairs={{0,8},{4,12},{8,0},{12,4},{16,24},{20,28},{24,16},{28,20},{1,9},{5... | collective-permute-start | bytes 116744 | tf_op jit(solution)/shard_map/ppermute | solution.py:649
  16.0 100.4 %collective-permute-start.16 = (bf16[608,768]{1,0:T(8,128)(2,1)S(1)}, bf16[608,768]{1,0:T(8,128)(2,1)}, u32[]{:S(2)}, u32[]{:S(2)}) collective-permute-start(bf16[608,768]{1,0:T(8,128)(2,1)S(1)} %spread_rows.1), channel_id=1, source_target_pairs={{0,2},{1,3},{2,0},{3,1},{4,6},{5,7},{6,4},{7,5},{8,10},{9,11},{10,... | collective-permute-start | bytes 2801672 | tf_op jit(solution)/shard_map/ppermute | solution.py:649
  40.8 27.6 %collective-permute-start.8 = (bf16[608,768]{1,0:T(8,128)(2,1)S(1)}, bf16[608,768]{1,0:T(8,128)(2,1)}, u32[]{:S(2)}, u32[]{:S(2)}) collective-permute-start(bf16[608,768]{1,0:T(8,128)(2,1)S(1)} %spread_rows.1), channel_id=1, source_target_pairs={{0,8},{4,12},{8,0},{12,4},{16,24},{20,28},{24,16},{28,20},{1,9},{5... | collective-permute-start | bytes 2801672 | tf_op jit(solution)/shard_map/ppermute | solution.py:649
  75.0 41.4 %collective-permute-start.11 = (bf16[4,2,96,768]{3,2,1,0:T(8,128)(2,1)}, bf16[4,2,96,768]{3,2,1,0:T(8,128)(2,1)}, u32[]{:S(2)}, u32[]{:S(2)}) collective-permute-start(bf16[4,2,96,768]{3,2,1,0:T(8,128)(2,1)} %get-tuple-element.126), channel_id=1, source_target_pairs={{0,8},{4,12},{8,0},{12,4},{16,24},{20,28},{24,16},{28,20},{1,9},{5... | collective-permute-start | bytes 3538952 | tf_op jit(solution)/shard_map/ppermute | solution.py:649
  75.3 41.1 %collective-permute-start.13 = (bf16[4,2,96,768]{3,2,1,0:T(8,128)(2,1)}, bf16[4,2,96,768]{3,2,1,0:T(8,128)(2,1)}, u32[]{:S(2)}, u32[]{:S(2)}) collective-permute-start(bf16[4,2,96,768]{3,2,1,0:T(8,128)(2,1)} %get-tuple-element.128.refs_3_), channel_id=1, source_target_pairs={{0,4},{4,0},{8,12},{12,8},{16,20},{20,16},{24,28},{28,24},{1,5},{5... | collective-permute-start | bytes 3538952 | tf_op jit(solution)/shard_map/ppermute | solution.py:649
  79.4 34.8 %collective-permute-start.12 = (bf16[2,2,96,768]{3,2,1,0:T(8,128)(2,1)}, bf16[2,2,96,768]{3,2,1,0:T(8,128)(2,1)S(1)}, u32[]{:S(2)}, u32[]{:S(2)}) collective-permute-start(bf16[2,2,96,768]{3,2,1,0:T(8,128)(2,1)} %slice.290), channel_id=1, source_target_pairs={{0,16},{4,20},{8,24},{12,28},{16,0},{20,4},{24,8},{28,12},{1,17},{... | collective-permute-start | bytes 1769480 | tf_op jit(solution)/shard_map/ppermute | solution.py:649
  82.1 32.1 %collective-permute-start.14 = (bf16[608,768]{1,0:T(8,128)(2,1)}, bf16[608,768]{1,0:T(8,128)(2,1)S(1)}, u32[]{:S(2)}, u32[]{:S(2)}) collective-permute-start(bf16[608,768]{1,0:T(8,128)(2,1)} %collective-permute-done.8), channel_id=1, source_target_pairs={{0,2},{1,3},{2,0},{3,1},{4,6},{5,7},{6,4},{7,5},{8,10},{9,11},{10,... | collective-permute-start | bytes 2801672 | tf_op jit(solution)/shard_map/ppermute | solution.py:649
  118.3 29.4 %collective-permute-start.20 = (bf16[4,2,96,768]{3,2,1,0:T(8,128)(2,1)}, bf16[4,2,96,768]{3,2,1,0:T(8,128)(2,1)}, u32[]{:S(2)}, u32[]{:S(2)}) collective-permute-start(bf16[4,2,96,768]{3,2,1,0:T(8,128)(2,1)} %collective-permute-done.11.refs_4_), channel_id=1, source_target_pairs={{0,4},{4,0},{8,12},{12,8},{16,20},{20,16},{24,28},{28,24},{1,5},{5... | collective-permute-start | bytes 3538952 | tf_op jit(solution)/shard_map/ppermute | solution.py:649
  118.6 29.1 %collective-permute-start.18 = (bf16[608,768]{1,0:T(8,128)(2,1)S(1)}, bf16[608,768]{1,0:T(8,128)(2,1)S(1)}, u32[]{:S(2)}, u32[]{:S(2)}) collective-permute-start(bf16[608,768]{1,0:T(8,128)(2,1)S(1)} %get-tuple-element.130.refs_1_), channel_id=1, source_target_pairs={{0,8},{4,12},{8,0},{12,4},{16,24},{20,28},{24,16},{28,20},{1,9},{5... | collective-permute-start | bytes 2801672 | tf_op jit(solution)/shard_map/ppermute | solution.py:649
  120.0 27.7 %collective-permute-start.19 = (bf16[608,768]{1,0:T(8,128)(2,1)S(1)}, bf16[608,768]{1,0:T(8,128)(2,1)S(1)}, u32[]{:S(2)}, u32[]{:S(2)}) collective-permute-start(bf16[608,768]{1,0:T(8,128)(2,1)S(1)} %get-tuple-element.130.refs_1_), channel_id=1, source_target_pairs={{0,2},{1,3},{2,0},{3,1},{4,6},{5,7},{6,4},{7,5},{8,10},{9,11},{10,... | collective-permute-start | bytes 2801672 | tf_op jit(solution)/shard_map/ppermute | solution.py:649
  120.6 26.0 %collective-permute-start.21 = (bf16[1,2,96,768]{3,2,1,0:T(8,128)(2,1)S(1)}, bf16[1,2,96,768]{3,2,1,0:T(8,128)(2,1)S(1)}, u32[]{:S(2)}, u32[]{:S(2)}) collective-permute-start(bf16[1,2,96,768]{3,2,1,0:T(8,128)(2,1)S(1)} %copy-done.43), channel_id=1, source_target_pairs={{0,16},{4,20},{8,24},{12,28},{16,0},{20,4},{24,8},{28,12},{1,17},{... | collective-permute-start | bytes 884744 | tf_op jit(solution)/shard_map/ppermute | solution.py:649
  147.7 29.9 %collective-permute-start.22 = (bf16[608,768]{1,0:T(8,128)(2,1)S(1)}, bf16[608,768]{1,0:T(8,128)(2,1)S(1)}, u32[]{:S(2)}, u32[]{:S(2)}) collective-permute-start(bf16[608,768]{1,0:T(8,128)(2,1)S(1)} %collective-permute-done.18.refs_3_), channel_id=1, source_target_pairs={{0,2},{1,3},{2,0},{3,1},{4,6},{5,7},{6,4},{7,5},{8,10},{9,11},{10,... | collective-permute-start | bytes 2801672 | tf_op jit(solution)/shard_map/ppermute | solution.py:649
  149.7 27.9 %collective-permute-start.15 = (bf16[2,2,96,768]{3,2,1,0:T(8,128)(2,1)S(1)}, bf16[2,2,96,768]{3,2,1,0:T(8,128)(2,1)S(1)}, u32[]{:S(2)}, u32[]{:S(2)}) collective-permute-start(bf16[2,2,96,768]{3,2,1,0:T(8,128)(2,1)S(1)} %get-tuple-element.131), channel_id=1, source_target_pairs={{0,16},{4,20},{8,24},{12,28},{16,0},{20,4},{24,8},{28,12},{1,17},{... | collective-permute-start | bytes 1769480 | tf_op jit(solution)/shard_map/ppermute | solution.py:649
  152.2 27.1 %collective-permute-start.28 = (bf16[4,2,96,768]{3,2,1,0:T(8,128)(2,1)S(1)}, bf16[4,2,96,768]{3,2,1,0:T(8,128)(2,1)S(1)}, u32[]{:S(2)}, u32[]{:S(2)}) collective-permute-start(bf16[4,2,96,768]{3,2,1,0:T(8,128)(2,1)S(1)} %constant_dynamic-update-slice_fusion.refs_5_), channel_id=1, source_target_pairs={{0,4},{4,0},{8,12},{12,8},{16,20},{20,16},{24,28},{28,24},{1,5},{5... | collective-permute-start | bytes 3538952 | tf_op jit(solution)/shard_map/ppermute | solution.py:649
  153.9 27.2 %collective-permute-start.25 = (bf16[608,768]{1,0:T(8,128)(2,1)S(1)}, bf16[608,768]{1,0:T(8,128)(2,1)S(1)}, u32[]{:S(2)}, u32[]{:S(2)}) collective-permute-start(bf16[608,768]{1,0:T(8,128)(2,1)S(1)} %collective-permute-done.18.refs_3_), channel_id=1, source_target_pairs={{0,1},{1,0},{2,3},{3,2},{4,5},{5,4},{6,7},{7,6},{8,9},{9,8},{10,11... | collective-permute-start | bytes 2801672 | tf_op jit(solution)/shard_map/ppermute | solution.py:649
  179.3 28.5 %collective-permute-start.27 = (bf16[2,2,96,768]{3,2,1,0:T(8,128)(2,1)S(1)}, bf16[2,2,96,768]{3,2,1,0:T(8,128)(2,1)}, u32[]{:S(2)}, u32[]{:S(2)}) collective-permute-start(bf16[2,2,96,768]{3,2,1,0:T(8,128)(2,1)S(1)} %get-tuple-element.138), channel_id=1, source_target_pairs={{0,16},{4,20},{8,24},{12,28},{16,0},{20,4},{24,8},{28,12},{1,17},{... | collective-permute-start | bytes 1769480 | tf_op jit(solution)/shard_map/ppermute | solution.py:649
  179.5 29.4 %collective-permute-start.29 = (bf16[2,2,96,768]{3,2,1,0:T(8,128)(2,1)S(1)}, bf16[2,2,96,768]{3,2,1,0:T(8,128)(2,1)}, u32[]{:S(2)}, u32[]{:S(2)}) collective-permute-start(bf16[2,2,96,768]{3,2,1,0:T(8,128)(2,1)S(1)} %collective-permute-done.15.refs_6_), channel_id=1, source_target_pairs={{0,4},{4,0},{8,12},{12,8},{16,20},{20,16},{24,28},{28,24},{1,5},{5... | collective-permute-start | bytes 1769480 | tf_op jit(solution)/shard_map/ppermute | solution.py:649
  207.9 34.8 %collective-permute-start.30 = (bf16[2,2,96,768]{3,2,1,0:T(8,128)(2,1)}, bf16[2,2,96,768]{3,2,1,0:T(8,128)(2,1)S(1)}, u32[]{:S(2)}, u32[]{:S(2)}) collective-permute-start(bf16[2,2,96,768]{3,2,1,0:T(8,128)(2,1)} %collective-permute-done.27.refs_6_), channel_id=1, source_target_pairs={{0,4},{4,0},{8,12},{12,8},{16,20},{20,16},{24,28},{28,24},{1,5},{5... | collective-permute-start | bytes 1769480 | tf_op jit(solution)/shard_map/ppermute | solution.py:649
  242.7 35.0 %collective-permute-start.31 = (bf16[2,384,768]{2,1,0:T(8,128)(2,1)}, bf16[2,384,768]{2,1,0:T(8,128)(2,1)}, u32[]{:S(2)}, u32[]{:S(2)}) collective-permute-start(bf16[2,384,768]{2,1,0:T(8,128)(2,1)} %get-tuple-element.151), channel_id=1, source_target_pairs={{0,4},{4,0},{8,12},{12,8},{16,20},{20,16},{24,28},{28,24},{1,5},{5... | collective-permute-start | bytes 3538952 | tf_op jit(solution)/shard_map/ppermute | solution.py:649
  277.7 27.7 %collective-permute-start.32 = (bf16[2,384,768]{2,1,0:T(8,128)(2,1)}, bf16[2,384,768]{2,1,0:T(8,128)(2,1)S(1)}, u32[]{:S(2)}, u32[]{:S(2)}) collective-permute-start(bf16[2,384,768]{2,1,0:T(8,128)(2,1)} %get-tuple-element.156), channel_id=1, source_target_pairs={{0,4},{4,0},{8,12},{12,8},{16,20},{20,16},{24,28},{28,24},{1,5},{5... | collective-permute-start | bytes 3538952 | tf_op jit(solution)/shard_map/ppermute | solution.py:649
  305.4 38.5 %collective-permute-start.35 = (bf16[2,384,768]{2,1,0:T(8,128)(2,1)S(1)}, bf16[2,384,768]{2,1,0:T(8,128)(2,1)}, u32[]{:S(2)}, u32[]{:S(2)}) collective-permute-start(bf16[2,384,768]{2,1,0:T(8,128)(2,1)S(1)} %copy-done.49), channel_id=1, source_target_pairs={{0,4},{4,0},{8,12},{12,8},{16,20},{20,16},{24,28},{28,24},{1,5},{5... | collective-permute-start | bytes 3538952 | tf_op jit(solution)/shard_map/ppermute | solution.py:649
  316.6 27.3 %collective-permute-start.36 = (bf16[608,768]{1,0:T(8,128)(2,1)S(1)}, bf16[608,768]{1,0:T(8,128)(2,1)}, u32[]{:S(2)}, u32[]{:S(2)}) collective-permute-start(bf16[608,768]{1,0:T(8,128)(2,1)S(1)} %get-tuple-element.281), channel_id=1, source_target_pairs={{0,2},{1,3},{2,0},{3,1},{4,6},{5,7},{6,4},{7,5},{8,10},{9,11},{10,... | collective-permute-start | bytes 2801672 | tf_op jit(solution)/shard_map/ppermute | solution.py:649
  318.2 25.7 %collective-permute-start.37 = (bf16[2,192,768]{2,1,0:T(8,128)(2,1)S(1)}, bf16[2,192,768]{2,1,0:T(8,128)(2,1)S(1)}, u32[]{:S(2)}, u32[]{:S(2)}) collective-permute-start(bf16[2,192,768]{2,1,0:T(8,128)(2,1)S(1)} %slice_add_fusion.11), channel_id=1, source_target_pairs={{0,16},{4,20},{8,24},{12,28},{16,0},{20,4},{24,8},{28,12},{1,17},{... | collective-permute-start | bytes 1769480 | tf_op jit(solution)/shard_map/ppermute | solution.py:649
  348.8 32.5 %collective-permute-start.40 = (bf16[608,768]{1,0:T(8,128)(2,1)S(1)}, bf16[608,768]{1,0:T(8,128)(2,1)S(1)}, u32[]{:S(2)}, u32[]{:S(2)}) collective-permute-start(bf16[608,768]{1,0:T(8,128)(2,1)S(1)} %fusion.10), channel_id=1, source_target_pairs={{0,8},{4,12},{8,0},{12,4},{16,24},{20,28},{24,16},{28,20},{1,9},{5... | collective-permute-start | bytes 2801672 | tf_op jit(solution)/shard_map/ppermute | solution.py:649
  354.3 55.3 %collective-permute-start.41 = (bf16[2,608,768]{2,1,0:T(8,128)(2,1)S(1)}, bf16[2,608,768]{2,1,0:T(8,128)(2,1)}, u32[]{:S(2)}, u32[]{:S(2)}) collective-permute-start(bf16[2,608,768]{2,1,0:T(8,128)(2,1)S(1)} %pad_maximum_fusion.1), channel_id=1, source_target_pairs={{0,2},{1,3},{2,0},{3,1},{4,6},{5,7},{6,4},{7,5},{8,10},{9,11},{10,... | collective-permute-start | bytes 5603336 | tf_op jit(solution)/shard_map/ppermute | solution.py:649
  356.7 46.0 %collective-permute-start.44 = (bf16[2,384,768]{2,1,0:T(8,128)(2,1)}, bf16[2,384,768]{2,1,0:T(8,128)(2,1)S(1)}, u32[]{:S(2)}, u32[]{:S(2)}) collective-permute-start(bf16[2,384,768]{2,1,0:T(8,128)(2,1)} %get-tuple-element.185), channel_id=1, source_target_pairs={{0,4},{4,0},{8,12},{12,8},{16,20},{20,16},{24,28},{28,24},{1,5},{5... | collective-permute-start | bytes 3538952 | tf_op jit(solution)/shard_map/ppermute | solution.py:649
  360.1 42.6 %collective-permute-start.42 = (bf16[2,192,768]{2,1,0:T(8,128)(2,1)S(1)}, bf16[2,192,768]{2,1,0:T(8,128)(2,1)}, u32[]{:S(2)}, u32[]{:S(2)}) collective-permute-start(bf16[2,192,768]{2,1,0:T(8,128)(2,1)S(1)} %slice_add_fusion.10), channel_id=1, source_target_pairs={{0,16},{4,20},{8,24},{12,28},{16,0},{20,4},{24,8},{28,12},{1,17},{... | collective-permute-start | bytes 1769480 | tf_op jit(solution)/shard_map/ppermute | solution.py:649
  369.8 32.9 %collective-permute-start.43 = (bf16[2,2,96,768]{3,2,0,1:T(8,128)(2,1)}, bf16[2,2,96,768]{3,2,0,1:T(8,128)(2,1)S(1)}, u32[]{:S(2)}, u32[]{:S(2)}) collective-permute-start(bf16[2,2,96,768]{3,2,0,1:T(8,128)(2,1)} %fusion.21), channel_id=1, source_target_pairs={{0,8},{4,12},{8,0},{12,4},{16,24},{20,28},{24,16},{28,20},{1,9},{5... | collective-permute-start | bytes 1769480 | tf_op jit(solution)/shard_map/ppermute | solution.py:649
  409.6 29.6 %collective-permute-start.47 = (bf16[2,192,768]{2,1,0:T(8,128)(2,1)S(1)}, bf16[2,192,768]{2,1,0:T(8,128)(2,1)}, u32[]{:S(2)}, u32[]{:S(2)}) collective-permute-start(bf16[2,192,768]{2,1,0:T(8,128)(2,1)S(1)} %slice_add_fusion.8), channel_id=1, source_target_pairs={{0,16},{4,20},{8,24},{12,28},{16,0},{20,4},{24,8},{28,12},{1,17},{... | collective-permute-start | bytes 1769480 | tf_op jit(solution)/shard_map/ppermute | solution.py:649
  412.9 37.1 %collective-permute-start.46 = (bf16[8,96,768]{2,1,0:T(8,128)(2,1)S(1)}, bf16[8,96,768]{2,1,0:T(8,128)(2,1)S(1)}, u32[]{:S(2)}, u32[]{:S(2)}) collective-permute-start(bf16[8,96,768]{2,1,0:T(8,128)(2,1)S(1)} %add.180), channel_id=1, source_target_pairs={{0,2},{1,3},{2,0},{3,1},{4,6},{5,7},{6,4},{7,5},{8,10},{9,11},{10,... | collective-permute-start | bytes 3538952 | tf_op jit(solution)/shard_map/ppermute | solution.py:649
  414.8 35.2 %collective-permute-start.48 = (bf16[608,768]{1,0:T(8,128)(2,1)S(1)}, bf16[608,768]{1,0:T(8,128)(2,1)S(1)}, u32[]{:S(2)}, u32[]{:S(2)}) collective-permute-start(bf16[608,768]{1,0:T(8,128)(2,1)S(1)} %bitcast_add_fusion.1), channel_id=1, source_target_pairs={{0,8},{4,12},{8,0},{12,4},{16,24},{20,28},{24,16},{28,20},{1,9},{5... | collective-permute-start | bytes 2801672 | tf_op jit(solution)/shard_map/ppermute | solution.py:649
  469.0 37.8 %all-to-all-start = ((bf16[8,112,768]{2,1,0:T(8,128)(2,1)}), bf16[8,112,768]{2,1,0:T(8,128)(2,1)S(1)}, u32[]{:S(2)}, u32[]{:S(2)}) async-start(bf16[8,112,768]{2,1,0:T(8,128)(2,1)} %fusion), calls=%async_computation | async-start | bytes 2752512 | tf_op jit(solution)/shard_map/all_to_all | solution.py:863
  (76 other events, 769.6 us)
where the time goes:
time: 520 us; the launch traced here: 511 us
  Pallas kernels  203 us (39%)
  waiting for transfers between devices  175 us (34%)
  starting transfers between devices  51.5 us (10%)
  other arithmetic  48.7 us (9%)
  local copies, waits for them, and re-layouts  30.2 us (6%)
    ppermute x52, waiting for transfers between devices, along(): return lambda value: lax.ppermute(value, axis, pairs)  151 us
    pallas_call x2, Pallas kernels, expert_math(): pl.pallas_call(expert_kernel, grid=(experts,), out_shape=(sds((experts, l...  67.7 us
    ppermute x52, starting transfers between devices, along(): return lambda value: lax.ppermute(value, axis, pairs)  44.9 us
    pallas_call x2, Pallas kernels, combine(): pl.pallas_call(functools.partial(combine_kernel, gated, len(sources)), gr...  37.3 us
    pallas_call x2, Pallas kernels, dispatch(): pl.pallas_call(functools.partial(dispatch_kernel, gated), grid=(experts,)...  32.8 us
    all_to_all x1, waiting for transfers between devices, body(): total = lax.all_to_all(total, 'dp', 0, 0, tiled=True)  23.3 us
    pallas_call x1, Pallas kernels, attention_forward(): pl.pallas_call(functools.partial(attention_forward_kernel, images, stride...  22.1 us
    pallas_call x1, Pallas kernels, attention_backward(): pl.pallas_call(functools.partial(attention_backward_kernel, images, strid...  21.4 us
  transfers between devices with their start and end apart: 54, of which 30 were waited for; matrix products, arithmetic and copies ran while one was open for 13% of the time, Pallas kernels for 40%

commit v1 on v0

--- a/solution.py
+++ b/solution.py
@@ -525,7 +525,14 @@
         steps.append((start - first + number + WINDOW - 1) // WINDOW)
         window[e * WINDOW : (e + 1) * WINDOW, :] = source_refs[e // per_source][e % per_source, pl.ds(first, WINDOW), :]
         parts.append(chosen(e, first))
-    total = dot(jnp.concatenate(parts, 1), window[...]).astype(BF16)
+    middle = padded // 32 * 16
+    total = jnp.concatenate(
+        [
+            dot(jnp.concatenate([part[rows] for part in parts], 1), window[...]).astype(BF16)
+            for rows in (slice(0, middle), slice(middle, padded))
+        ],
+        0,
+    )
 
     def finish(ref):
         ref[0] = total
@@ -844,7 +851,6 @@
     others = jnp.broadcast_to(extra_y.astype(F32) + extra_far.astype(F32), (OUTER, EXTRA, features))
     others = jnp.concatenate((upper.astype(F32), others), 1)
     total = (keep.astype(F32) + near.astype(F32) + others).astype(BF16)
-    total, low_1 = lax.optimization_barrier((total, low_1))
     block_output = finish(residual, (mixture[0], mixture_y[0], mixture_low), tokens, images, stride)
 
     own_share = jnp.concatenate((mine_0[:, :, :block], mine_1[:, :, :block]), 0)

time: 520 us -> 518 us (level)
  Pallas kernels: 203 us -> 193 us
  waiting for transfers between devices: 175 us -> 182 us
    ppermute x52, waiting for transfers between devices: 151 us -> 181 us  [along(): return lambda value: lax.ppermute(value, axis, pairs)]
    all_to_all x1, waiting for transfers between devices: 23.3 us -> 0.01 us  [body(): total = lax.all_to_all(total, 'dp', 0, 0, tiled=True)]
    pallas_call x2, Pallas kernels: 67.7 us -> 60.6 us  [expert_math(): pl.pallas_call(expert_kernel, grid=(experts,), out_shape=(sds((experts, l...]
  transfers between devices with their start and end apart: 54 -> 54, of which waited for: 30 -> 28; matrix products, arithmetic and copies ran while one was open for 13% -> 13% of each run, Pallas kernels for 40% -> 38%
where the time goes in v1:
time: 518 us; the launch traced here: 509 us
  Pallas kernels  193 us (37%)
  waiting for transfers between devices  182 us (35%)
  starting transfers between devices  50.6 us (10%)
  other arithmetic  48.9 us (9%)
  local copies, waits for them, and re-layouts  31 us (6%)
    ppermute x52, waiting for transfers between devices, along(): return lambda value: lax.ppermute(value, axis, pairs)  181 us
    pallas_call x2, Pallas kernels, expert_math(): pl.pallas_call(expert_kernel, grid=(experts,), out_shape=(sds((experts, l...  60.6 us
    ppermute x52, starting transfers between devices, along(): return lambda value: lax.ppermute(value, axis, pairs)  45.7 us
    pallas_call x2, Pallas kernels, combine(): pl.pallas_call(functools.partial(combine_kernel, gated, len(sources)), gr...  34.8 us
    pallas_call x2, Pallas kernels, dispatch(): pl.pallas_call(functools.partial(dispatch_kernel, gated), grid=(experts,)...  32.8 us
    pallas_call x1, Pallas kernels, attention_forward(): pl.pallas_call(functools.partial(attention_forward_kernel, images, stride...  22.1 us
    pallas_call x1, Pallas kernels, attention_backward(): pl.pallas_call(functools.partial(attention_backward_kernel, images, strid...  21.4 us
    pallas_call x1, Pallas kernels, attention_rest(): pl.pallas_call(functools.partial(attention_rest_kernel, images, stride, h...  19.5 us
  transfers between devices with their start and end apart: 54, of which 28 were waited for; matrix products, arithmetic and copies ran while one was open for 13% of the time, Pallas kernels for 38%

profile of v1, /device:TPU:0, one launch (start us, length us, event | category | flops | bytes accessed | tf_op | source)
XLA Modules:
  0.0 508.9 jit_solution(1396816098562195063)
XLA Ops:
  2.4 3.1 collective-permute-start
  25.3 8.1 %collective-permute-done.2 = bf16[2,112,768]{2,1,0:T(8,128)(2,1)S(1)} collective-permute-done((bf16[2,112,768]{2,1,0:T(8,128)(2,1)S(1)}, bf16[2,112,768]{2,1,0:T(8,128)(2,1)S(1)}, u32[]{:S(2)}, u32[]{:S(2)}) %collective-permute-start.2) | collective-permute-done | bytes 344096 | tf_op jit(solution)/shard_map/ppermute | solution.py:656
  42.6 9.6 %collective-permute-done.3 = bf16[4,112,768]{2,1,0:T(8,128)(2,1)S(1)} collective-permute-done((bf16[4,112,768]{2,1,0:T(8,128)(2,1)}, bf16[4,112,768]{2,1,0:T(8,128)(2,1)S(1)}, u32[]{:S(2)}, u32[]{:S(2)}) %collective-permute-start.3) | collective-permute-done | bytes 688160 | tf_op jit(solution)/shard_map/ppermute | solution.py:656
  61.6 4.1 collective-permute-done.6
  79.4 2.7 collective-permute-start.12
  82.6 22.1 %attention_forward.1 = (f32[608,768]{1,0:T(8,128)}, bf16[608,768]{1,0:T(8,128)(2,1)S(1)}, bf16[608,768]{1,0:T(8,128)(2,1)S(1)}, bf16[4,768,768]{2,1,0:T(8,128)(2...) custom-call(s32[1]{0:T(128)} %bitcast.refs_0_, f32[591,768]{1,0:T(8,128)} %refs_0_.3, ...), custom_call_target="tpu_custom_call" | custom-call | flops 11000000512 | tf_op jit(solution)/shard_map/attention_forward/pallas_call | solution.py:145
  105.6 8.6 %collective-permute-done.12 = bf16[2,2,96,768]{3,2,1,0:T(8,128)(2,1)S(1)} collective-permute-done((bf16[2,2,96,768]{3,2,1,0:T(8,128)(2,1)}, bf16[2,2,96,768]{3,2,1,0:T(8,128)(2,1)S(1)}, u32[]{:S(2)}, u32[]{:S(2)}) %collective-permute-start.12) | collective-permute-done | bytes 589856 | tf_op jit(solution)/shard_map/ppermute | solution.py:656
  122.0 2.9 collective-permute-done.17.refs_2_
  124.9 17.2 %dispatch_gated.1.refs_2_ = bf16[4,2064,768]{2,1,0:T(8,128)(2,1)} custom-call(s32[68]{0:T(128)S(1)} %copy-done.3, bf16[4,608,768]{2,1,0:T(8,128)(2,1)S(1)} %pad_maximum_fusion.refs_1_, bf16[4,608,768]{2,1,0:T(8,128)(2,1)} %collective-permute-done.17.refs_2_, s32[4,8,608]{2,1,0:T(8,128)S(1)} %copy-done.2, f32[4,8,608]{2,1,0:T(8,128)S(1)} %fusion.22.refs_4_), custom_call_target="tpu_custom_call" | custom-call | flops 7500000256 | tf_op jit(solution)/shard_map/dispatch_gated/pallas_call | solution.py:391
  142.1 4.5 collective-permute-done.21
  154.4 23.2 %collective-permute-done.15.refs_6_ = bf16[2,2,96,768]{3,2,1,0:T(8,128)(2,1)S(1)} collective-permute-done((bf16[2,2,96,768]{3,2,1,0:T(8,128)(2,1)S(1)}, bf16[2,2,96,768]{3,2,1,0:T(8,128)(2,1)S(1)}, u32[]{:S(2)}, u32[]{:S(2)}) %collective-permute-start.15) | collective-permute-done | bytes 589856 | tf_op jit(solution)/shard_map/ppermute | solution.py:656
  183.0 15.6 %dispatch.1.refs_1_ = bf16[4,2064,768]{2,1,0:T(8,128)(2,1)} custom-call(s32[68]{0:T(128)S(1)} %copy-done.3, bf16[608,768]{1,0:T(8,128)(2,1)S(1)} %get-tuple-element.128.refs_1_, bf16[608,768]{1,0:T(8,128)(2,1)S(1)} %collective-permute-done.19.refs_2_, bf16[608,768]{1,0:T(8,128)(2,1)S(1)} %collective-permute-done.18.refs_3_, ...), custom_call_target="tpu_custom_call" | custom-call | flops 7500000256 | tf_op jit(solution)/shard_map/dispatch/pallas_call | solution.py:391
  198.6 9.2 %collective-permute-done.27.refs_6_ = bf16[2,2,96,768]{3,2,1,0:T(8,128)(2,1)} collective-permute-done((bf16[2,2,96,768]{3,2,1,0:T(8,128)(2,1)S(1)}, bf16[2,2,96,768]{3,2,1,0:T(8,128)(2,1)}, u32[]{:S(2)}, u32[]{:S(2)}) %collective-permute-start.27) | collective-permute-done | bytes 589856 | tf_op jit(solution)/shard_map/ppermute | solution.py:656
  208.9 29.1 %expert_math.2 = (bf16[2,2064,768]{2,1,0:T(8,128)(2,1)}, bf16[2,2064,768]{2,1,0:T(8,128)(2,1)}, bf16[2,384,768]{2,1,0:T(8,128)(2,1)}, bf16[2,384,768]{2,1,0:T(8,...) custom-call(s32[3]{0:T(128)} %pad_add_fusion.refs_0_, bf16[4,2064,768]{2,1,0:T(8,128)(2,1)} %dispatch.1.refs_1_, ...), custom_call_target="tpu_custom_call" | custom-call | flops 16499999744 | tf_op jit(solution)/shard_map/expert_math/pallas_call | solution.py:478
  239.1 31.6 %expert_math.3 = (bf16[2,2064,768]{2,1,0:T(8,128)(2,1)}, bf16[2,2064,768]{2,1,0:T(8,128)(2,1)}, bf16[2,384,768]{2,1,0:T(8,128)(2,1)}, bf16[2,384,768]{2,1,0:T(8,...) custom-call(s32[3]{0:T(128)} %pad_add_fusion.1.refs_0_, bf16[4,2064,768]{2,1,0:T(8,128)(2,1)} %dispatch.1.refs_1_, ...), custom_call_target="tpu_custom_call" | custom-call | flops 16499999744 | tf_op jit(solution)/shard_map/expert_math/pallas_call | solution.py:478
  270.6 5.8 %collective-permute-start.32 = (bf16[2,384,768]{2,1,0:T(8,128)(2,1)}, bf16[2,384,768]{2,1,0:T(8,128)(2,1)S(1)}, u32[]{:S(2)}, u32[]{:S(2)}) collective-permute-start(bf16[2,384,768]{2,1,0:T(8,128)(2,1)} %get-tuple-element.154), channel_id=1, source_target_pairs={{0,4},{4,0},{8,12},{12,8},{16,20},{20,16},{24,28},{28,24},{1,5},{5... | collective-permute-start | bytes 3538952 | tf_op jit(solution)/shard_map/ppermute | solution.py:656
  277.8 16.8 %combine.1 = (bf16[4,608,768]{2,1,0:T(8,128)(2,1)}, bf16[4,608,768]{2,1,0:T(8,128)(2,1)}) custom-call(s32[68]{0:T(128)S(1)} %copy-done.3, bf16[2,2064,768]{2,1,0:T(8,128)(2,1)} %get-tuple-element.145.refs_1_, bf16[2,2064,768]{2,1,0:T(8,128)(2,1)} %get-tuple-element.150.refs_2_, s32[8,608,4]{2,1,0:T(8,128)S(1)} %fusion.2.refs_3_), custom_call_target="tpu_custom_call" | custom-call | flops 1000000000 | tf_op jit(solution)/shard_map/combine/pallas_call | solution.py:565
  294.7 11.1 %collective-permute-done.33 = bf16[2,192,768]{2,1,0:T(8,128)(2,1)S(1)} collective-permute-done((bf16[2,192,768]{2,1,0:T(8,128)(2,1)S(1)}, bf16[2,192,768]{2,1,0:T(8,128)(2,1)S(1)}, u32[]{:S(2)}, u32[]{:S(2)}) %collective-permute-start.33) | collective-permute-done | bytes 589856 | tf_op jit(solution)/shard_map/ppermute | solution.py:656
  306.2 6.3 %collective-permute-done.34 = bf16[4,608,768]{2,1,0:T(8,128)(2,1)S(1)} collective-permute-done((bf16[4,608,768]{2,1,0:T(8,128)(2,1)}, bf16[4,608,768]{2,1,0:T(8,128)(2,1)S(1)}, u32[]{:S(2)}, u32[]{:S(2)}) %collective-permute-start.34) | collective-permute-done | bytes 3735584 | tf_op jit(solution)/shard_map/ppermute | solution.py:656
  312.6 4.4 fusion.11
  318.7 17.9 %combine_gated.1 = (bf16[4,608,768]{2,1,0:T(8,128)(2,1)}, bf16[4,608,768]{2,1,0:T(8,128)(2,1)}) custom-call(s32[68]{0:T(128)S(1)} %copy-done.3, bf16[2,2064,768]{2,1,0:T(8,128)(2,1)} %get-tuple-element.159.refs_1_, bf16[2,2064,768]{2,1,0:T(8,128)(2,1)} %get-tuple-element.160.refs_2_, s32[8,608,4]{2,1,0:T(8,128)S(1)} %fusion.2.refs_3_, f32[8,608,4]{2,1,0:T(8,128)S(1)} %bitcast.92), custom_call_target="tpu_custom_call" | custom-call | flops 1000000000 | tf_op jit(solution)/shard_map/combine_gated/pallas_call | solution.py:565
  336.6 10.5 %collective-permute-done.37 = bf16[2,192,768]{2,1,0:T(8,128)(2,1)S(1)} collective-permute-done((bf16[2,192,768]{2,1,0:T(8,128)(2,1)S(1)}, bf16[2,192,768]{2,1,0:T(8,128)(2,1)S(1)}, u32[]{:S(2)}, u32[]{:S(2)}) %collective-permute-start.37) | collective-permute-done | bytes 589856 | tf_op jit(solution)/shard_map/ppermute | solution.py:656
  362.7 10.3 %collective-permute-done.39.refs_3_ = bf16[608,768]{1,0:T(8,128)(2,1)S(1)} collective-permute-done((bf16[608,768]{1,0:T(8,128)(2,1)}, bf16[608,768]{1,0:T(8,128)(2,1)S(1)}, u32[]{:S(2)}, u32[]{:S(2)}) %collective-permute-start.39) | collective-permute-done | bytes 933920 | tf_op jit(solution)/shard_map/ppermute | solution.py:656
  373.0 10.7 %collective-permute-done.40.refs_4_ = bf16[608,768]{1,0:T(8,128)(2,1)S(1)} collective-permute-done((bf16[608,768]{1,0:T(8,128)(2,1)S(1)}, bf16[608,768]{1,0:T(8,128)(2,1)S(1)}, u32[]{:S(2)}, u32[]{:S(2)}) %collective-permute-start.40) | collective-permute-done | bytes 933920 | tf_op jit(solution)/shard_map/ppermute | solution.py:656
  383.6 21.4 %attention_backward.1 = (bf16[8,96,768]{2,1,0:T(8,128)(2,1)}, bf16[8,96,768]{2,1,0:T(8,128)(2,1)}, f32[608,768]{1,0:T(8,128)}, bf16[608,768]{1,0:T(8,128)(2,1)S(...) custom-call(f32[591,768]{1,0:T(8,128)} %refs_0_.2, ...), custom_call_target="tpu_custom_call" | custom-call | flops 10000000000 | tf_op jit(solution)/shard_map/attention_backward/pallas_call | solution.py:287
  405.1 7.7 %collective-permute-done.41 = bf16[2,608,768]{2,1,0:T(8,128)(2,1)} collective-permute-done((bf16[2,608,768]{2,1,0:T(8,128)(2,1)S(1)}, bf16[2,608,768]{2,1,0:T(8,128)(2,1)}, u32[]{:S(2)}, u32[]{:S(2)}) %collective-permute-start.41) | collective-permute-done | bytes 1867808 | tf_op jit(solution)/shard_map/ppermute | solution.py:656
  412.9 2.9 collective-permute-done.45
  418.1 19.5 %attention_backward_rest.1 = (f32[591,768]{1,0:T(8,128)}, bf16[8,112,768]{2,1,0:T(8,128)(2,1)}, bf16[8,112,768]{2,1,0:T(8,128)(2,1)}, bf16[16,768]{1,0:T(8,128)(2,1)S(1)}) custom-call(f32[591,768]{1,0:T(8,128)} %refs_0_.3, f32[608,768]{1,0:T(8,128)} %get-tuple-element.185.refs_1_, bf16[608,768]{1,0:T(8,128)(2,1)S(1)} %get-tuple-element.186.refs_2_, ...), custom_call_target="tpu_custom_call" | custom-call | flops 10000000000 | tf_op jit(solution)/shard_map/attention_backward_rest/pallas_call | solution.py:307
  437.6 3.4 collective-permute-done.47
  441.0 12.3 %collective-permute-done.48.c_ref = bf16[608,768]{1,0:T(8,128)(2,1)S(1)} collective-permute-done((bf16[608,768]{1,0:T(8,128)(2,1)S(1)}, bf16[608,768]{1,0:T(8,128)(2,1)S(1)}, u32[]{:S(2)}, u32[]{:S(2)}) %collective-permute-start.48) | collective-permute-done | bytes 933920 | tf_op jit(solution)/shard_map/ppermute | solution.py:656
  460.1 3.6 all-to-all-start
  474.8 25.5 %collective-permute-done.52 = bf16[2,2,96,768]{3,2,0,1:T(8,128)(2,1)} collective-permute-done((bf16[2,2,96,768]{3,2,0,1:T(8,128)(2,1)}, bf16[2,2,96,768]{3,2,0,1:T(8,128)(2,1)}, u32[]{:S(2)}, u32[]{:S(2)}) %collective-permute-start.52) | collective-permute-done | bytes 589856 | tf_op jit(solution)/shard_map/ppermute | solution.py:656
  (304 shorter events, 125.7 us)
Async XLA Ops:
  2.4 38.0 %collective-permute-start = (f32[4,4,608]{2,1,0:T(4,128)S(1)}, f32[4,4,608]{2,1,0:T(4,128)S(1)}, u32[]{:S(2)}, u32[]{:S(2)}) collective-permute-start(f32[4,4,608]{2,1,0:T(4,128)S(1)} %pad.14), channel_id=1, source_target_pairs={{0,8},{4,12},{8,0},{12,4},{16,24},{20,28},{24,16},{28,20},{1,9},{5... | collective-permute-start | bytes 116744 | tf_op jit(solution)/shard_map/ppermute | solution.py:656
  16.0 100.4 %collective-permute-start.16 = (bf16[608,768]{1,0:T(8,128)(2,1)S(1)}, bf16[608,768]{1,0:T(8,128)(2,1)}, u32[]{:S(2)}, u32[]{:S(2)}) collective-permute-start(bf16[608,768]{1,0:T(8,128)(2,1)S(1)} %spread_rows.1), channel_id=1, source_target_pairs={{0,2},{1,3},{2,0},{3,1},{4,6},{5,7},{6,4},{7,5},{8,10},{9,11},{10,... | collective-permute-start | bytes 2801672 | tf_op jit(solution)/shard_map/ppermute | solution.py:656
  40.8 27.6 %collective-permute-start.8 = (bf16[608,768]{1,0:T(8,128)(2,1)S(1)}, bf16[608,768]{1,0:T(8,128)(2,1)}, u32[]{:S(2)}, u32[]{:S(2)}) collective-permute-start(bf16[608,768]{1,0:T(8,128)(2,1)S(1)} %spread_rows.1), channel_id=1, source_target_pairs={{0,8},{4,12},{8,0},{12,4},{16,24},{20,28},{24,16},{28,20},{1,9},{5... | collective-permute-start | bytes 2801672 | tf_op jit(solution)/shard_map/ppermute | solution.py:656
  75.0 41.4 %collective-permute-start.11 = (bf16[4,2,96,768]{3,2,1,0:T(8,128)(2,1)}, bf16[4,2,96,768]{3,2,1,0:T(8,128)(2,1)}, u32[]{:S(2)}, u32[]{:S(2)}) collective-permute-start(bf16[4,2,96,768]{3,2,1,0:T(8,128)(2,1)} %get-tuple-element.124), channel_id=1, source_target_pairs={{0,8},{4,12},{8,0},{12,4},{16,24},{20,28},{24,16},{28,20},{1,9},{5... | collective-permute-start | bytes 3538952 | tf_op jit(solution)/shard_map/ppermute | solution.py:656
  75.3 41.1 %collective-permute-start.13 = (bf16[4,2,96,768]{3,2,1,0:T(8,128)(2,1)}, bf16[4,2,96,768]{3,2,1,0:T(8,128)(2,1)}, u32[]{:S(2)}, u32[]{:S(2)}) collective-permute-start(bf16[4,2,96,768]{3,2,1,0:T(8,128)(2,1)} %get-tuple-element.126.refs_3_), channel_id=1, source_target_pairs={{0,4},{4,0},{8,12},{12,8},{16,20},{20,16},{24,28},{28,24},{1,5},{5... | collective-permute-start | bytes 3538952 | tf_op jit(solution)/shard_map/ppermute | solution.py:656
  79.4 34.8 %collective-permute-start.12 = (bf16[2,2,96,768]{3,2,1,0:T(8,128)(2,1)}, bf16[2,2,96,768]{3,2,1,0:T(8,128)(2,1)S(1)}, u32[]{:S(2)}, u32[]{:S(2)}) collective-permute-start(bf16[2,2,96,768]{3,2,1,0:T(8,128)(2,1)} %slice.290), channel_id=1, source_target_pairs={{0,16},{4,20},{8,24},{12,28},{16,0},{20,4},{24,8},{28,12},{1,17},{... | collective-permute-start | bytes 1769480 | tf_op jit(solution)/shard_map/ppermute | solution.py:656
  82.1 32.1 %collective-permute-start.14 = (bf16[608,768]{1,0:T(8,128)(2,1)}, bf16[608,768]{1,0:T(8,128)(2,1)S(1)}, u32[]{:S(2)}, u32[]{:S(2)}) collective-permute-start(bf16[608,768]{1,0:T(8,128)(2,1)} %collective-permute-done.8), channel_id=1, source_target_pairs={{0,2},{1,3},{2,0},{3,1},{4,6},{5,7},{6,4},{7,5},{8,10},{9,11},{10,... | collective-permute-start | bytes 2801672 | tf_op jit(solution)/shard_map/ppermute | solution.py:656
  118.3 29.4 %collective-permute-start.20 = (bf16[4,2,96,768]{3,2,1,0:T(8,128)(2,1)}, bf16[4,2,96,768]{3,2,1,0:T(8,128)(2,1)}, u32[]{:S(2)}, u32[]{:S(2)}) collective-permute-start(bf16[4,2,96,768]{3,2,1,0:T(8,128)(2,1)} %collective-permute-done.11.refs_4_), channel_id=1, source_target_pairs={{0,4},{4,0},{8,12},{12,8},{16,20},{20,16},{24,28},{28,24},{1,5},{5... | collective-permute-start | bytes 3538952 | tf_op jit(solution)/shard_map/ppermute | solution.py:656
  118.6 29.1 %collective-permute-start.18 = (bf16[608,768]{1,0:T(8,128)(2,1)S(1)}, bf16[608,768]{1,0:T(8,128)(2,1)S(1)}, u32[]{:S(2)}, u32[]{:S(2)}) collective-permute-start(bf16[608,768]{1,0:T(8,128)(2,1)S(1)} %get-tuple-element.128.refs_1_), channel_id=1, source_target_pairs={{0,8},{4,12},{8,0},{12,4},{16,24},{20,28},{24,16},{28,20},{1,9},{5... | collective-permute-start | bytes 2801672 | tf_op jit(solution)/shard_map/ppermute | solution.py:656
  120.0 27.7 %collective-permute-start.19 = (bf16[608,768]{1,0:T(8,128)(2,1)S(1)}, bf16[608,768]{1,0:T(8,128)(2,1)S(1)}, u32[]{:S(2)}, u32[]{:S(2)}) collective-permute-start(bf16[608,768]{1,0:T(8,128)(2,1)S(1)} %get-tuple-element.128.refs_1_), channel_id=1, source_target_pairs={{0,2},{1,3},{2,0},{3,1},{4,6},{5,7},{6,4},{7,5},{8,10},{9,11},{10,... | collective-permute-start | bytes 2801672 | tf_op jit(solution)/shard_map/ppermute | solution.py:656
  147.7 29.9 %collective-permute-start.22 = (bf16[608,768]{1,0:T(8,128)(2,1)S(1)}, bf16[608,768]{1,0:T(8,128)(2,1)S(1)}, u32[]{:S(2)}, u32[]{:S(2)}) collective-permute-start(bf16[608,768]{1,0:T(8,128)(2,1)S(1)} %collective-permute-done.18.refs_3_), channel_id=1, source_target_pairs={{0,2},{1,3},{2,0},{3,1},{4,6},{5,7},{6,4},{7,5},{8,10},{9,11},{10,... | collective-permute-start | bytes 2801672 | tf_op jit(solution)/shard_map/ppermute | solution.py:656
  149.7 27.9 %collective-permute-start.15 = (bf16[2,2,96,768]{3,2,1,0:T(8,128)(2,1)S(1)}, bf16[2,2,96,768]{3,2,1,0:T(8,128)(2,1)S(1)}, u32[]{:S(2)}, u32[]{:S(2)}) collective-permute-start(bf16[2,2,96,768]{3,2,1,0:T(8,128)(2,1)S(1)} %get-tuple-element.129), channel_id=1, source_target_pairs={{0,16},{4,20},{8,24},{12,28},{16,0},{20,4},{24,8},{28,12},{1,17},{... | collective-permute-start | bytes 1769480 | tf_op jit(solution)/shard_map/ppermute | solution.py:656
  153.9 27.2 %collective-permute-start.25 = (bf16[608,768]{1,0:T(8,128)(2,1)S(1)}, bf16[608,768]{1,0:T(8,128)(2,1)S(1)}, u32[]{:S(2)}, u32[]{:S(2)}) collective-permute-start(bf16[608,768]{1,0:T(8,128)(2,1)S(1)} %collective-permute-done.18.refs_3_), channel_id=1, source_target_pairs={{0,1},{1,0},{2,3},{3,2},{4,5},{5,4},{6,7},{7,6},{8,9},{9,8},{10,11... | collective-permute-start | bytes 2801672 | tf_op jit(solution)/shard_map/ppermute | solution.py:656
  179.3 28.5 %collective-permute-start.27 = (bf16[2,2,96,768]{3,2,1,0:T(8,128)(2,1)S(1)}, bf16[2,2,96,768]{3,2,1,0:T(8,128)(2,1)}, u32[]{:S(2)}, u32[]{:S(2)}) collective-permute-start(bf16[2,2,96,768]{3,2,1,0:T(8,128)(2,1)S(1)} %get-tuple-element.136), channel_id=1, source_target_pairs={{0,16},{4,20},{8,24},{12,28},{16,0},{20,4},{24,8},{28,12},{1,17},{... | collective-permute-start | bytes 1769480 | tf_op jit(solution)/shard_map/ppermute | solution.py:656
  179.5 29.4 %collective-permute-start.29 = (bf16[2,2,96,768]{3,2,1,0:T(8,128)(2,1)S(1)}, bf16[2,2,96,768]{3,2,1,0:T(8,128)(2,1)}, u32[]{:S(2)}, u32[]{:S(2)}) collective-permute-start(bf16[2,2,96,768]{3,2,1,0:T(8,128)(2,1)S(1)} %collective-permute-done.15.refs_6_), channel_id=1, source_target_pairs={{0,4},{4,0},{8,12},{12,8},{16,20},{20,16},{24,28},{28,24},{1,5},{5... | collective-permute-start | bytes 1769480 | tf_op jit(solution)/shard_map/ppermute | solution.py:656
  207.8 30.2 %collective-permute-start.30 = (bf16[2,2,96,768]{3,2,1,0:T(8,128)(2,1)}, bf16[2,2,96,768]{3,2,1,0:T(8,128)(2,1)S(1)}, u32[]{:S(2)}, u32[]{:S(2)}) collective-permute-start(bf16[2,2,96,768]{3,2,1,0:T(8,128)(2,1)} %collective-permute-done.27.refs_6_), channel_id=1, source_target_pairs={{0,4},{4,0},{8,12},{12,8},{16,20},{20,16},{24,28},{28,24},{1,5},{5... | collective-permute-start | bytes 1769480 | tf_op jit(solution)/shard_map/ppermute | solution.py:656
  238.0 32.6 %collective-permute-start.31 = (bf16[2,384,768]{2,1,0:T(8,128)(2,1)}, bf16[2,384,768]{2,1,0:T(8,128)(2,1)}, u32[]{:S(2)}, u32[]{:S(2)}) collective-permute-start(bf16[2,384,768]{2,1,0:T(8,128)(2,1)} %get-tuple-element.149), channel_id=1, source_target_pairs={{0,4},{4,0},{8,12},{12,8},{16,20},{20,16},{24,28},{28,24},{1,5},{5... | collective-permute-start | bytes 3538952 | tf_op jit(solution)/shard_map/ppermute | solution.py:656
  270.6 35.1 %collective-permute-start.32 = (bf16[2,384,768]{2,1,0:T(8,128)(2,1)}, bf16[2,384,768]{2,1,0:T(8,128)(2,1)S(1)}, u32[]{:S(2)}, u32[]{:S(2)}) collective-permute-start(bf16[2,384,768]{2,1,0:T(8,128)(2,1)} %get-tuple-element.154), channel_id=1, source_target_pairs={{0,4},{4,0},{8,12},{12,8},{16,20},{20,16},{24,28},{28,24},{1,5},{5... | collective-permute-start | bytes 3538952 | tf_op jit(solution)/shard_map/ppermute | solution.py:656
  277.7 28.0 %collective-permute-start.33 = (bf16[2,192,768]{2,1,0:T(8,128)(2,1)S(1)}, bf16[2,192,768]{2,1,0:T(8,128)(2,1)S(1)}, u32[]{:S(2)}, u32[]{:S(2)}) collective-permute-start(bf16[2,192,768]{2,1,0:T(8,128)(2,1)S(1)} %slice_add_fusion.9), channel_id=1, source_target_pairs={{0,16},{4,20},{8,24},{12,28},{16,0},{20,4},{24,8},{28,12},{1,17},{... | collective-permute-start | bytes 1769480 | tf_op jit(solution)/shard_map/ppermute | solution.py:656
  305.8 41.2 %collective-permute-start.35 = (bf16[2,384,768]{2,1,0:T(8,128)(2,1)S(1)}, bf16[2,384,768]{2,1,0:T(8,128)(2,1)}, u32[]{:S(2)}, u32[]{:S(2)}) collective-permute-start(bf16[2,384,768]{2,1,0:T(8,128)(2,1)S(1)} %copy-done.46), channel_id=1, source_target_pairs={{0,4},{4,0},{8,12},{12,8},{16,20},{20,16},{24,28},{28,24},{1,5},{5... | collective-permute-start | bytes 3538952 | tf_op jit(solution)/shard_map/ppermute | solution.py:656
  317.0 30.1 %collective-permute-start.36 = (bf16[608,768]{1,0:T(8,128)(2,1)S(1)}, bf16[608,768]{1,0:T(8,128)(2,1)}, u32[]{:S(2)}, u32[]{:S(2)}) collective-permute-start(bf16[608,768]{1,0:T(8,128)(2,1)S(1)} %get-tuple-element.277), channel_id=1, source_target_pairs={{0,2},{1,3},{2,0},{3,1},{4,6},{5,7},{6,4},{7,5},{8,10},{9,11},{10,... | collective-permute-start | bytes 2801672 | tf_op jit(solution)/shard_map/ppermute | solution.py:656
  318.6 28.5 %collective-permute-start.37 = (bf16[2,192,768]{2,1,0:T(8,128)(2,1)S(1)}, bf16[2,192,768]{2,1,0:T(8,128)(2,1)S(1)}, u32[]{:S(2)}, u32[]{:S(2)}) collective-permute-start(bf16[2,192,768]{2,1,0:T(8,128)(2,1)S(1)} %slice_add_fusion.11), channel_id=1, source_target_pairs={{0,16},{4,20},{8,24},{12,28},{16,0},{20,4},{24,8},{28,12},{1,17},{... | collective-permute-start | bytes 1769480 | tf_op jit(solution)/shard_map/ppermute | solution.py:656
  352.1 31.6 %collective-permute-start.40 = (bf16[608,768]{1,0:T(8,128)(2,1)S(1)}, bf16[608,768]{1,0:T(8,128)(2,1)S(1)}, u32[]{:S(2)}, u32[]{:S(2)}) collective-permute-start(bf16[608,768]{1,0:T(8,128)(2,1)S(1)} %fusion.10), channel_id=1, source_target_pairs={{0,8},{4,12},{8,0},{12,4},{16,24},{20,28},{24,16},{28,20},{1,9},{5... | collective-permute-start | bytes 2801672 | tf_op jit(solution)/shard_map/ppermute | solution.py:656
  357.4 55.3 %collective-permute-start.41 = (bf16[2,608,768]{2,1,0:T(8,128)(2,1)S(1)}, bf16[2,608,768]{2,1,0:T(8,128)(2,1)}, u32[]{:S(2)}, u32[]{:S(2)}) collective-permute-start(bf16[2,608,768]{2,1,0:T(8,128)(2,1)S(1)} %pad_maximum_fusion.1), channel_id=1, source_target_pairs={{0,2},{1,3},{2,0},{3,1},{4,6},{5,7},{6,4},{7,5},{8,10},{9,11},{10,... | collective-permute-start | bytes 5603336 | tf_op jit(solution)/shard_map/ppermute | solution.py:656
  359.9 45.1 %collective-permute-start.44 = (bf16[2,384,768]{2,1,0:T(8,128)(2,1)}, bf16[2,384,768]{2,1,0:T(8,128)(2,1)S(1)}, u32[]{:S(2)}, u32[]{:S(2)}) collective-permute-start(bf16[2,384,768]{2,1,0:T(8,128)(2,1)} %get-tuple-element.183), channel_id=1, source_target_pairs={{0,4},{4,0},{8,12},{12,8},{16,20},{20,16},{24,28},{28,24},{1,5},{5... | collective-permute-start | bytes 3538952 | tf_op jit(solution)/shard_map/ppermute | solution.py:656
  362.5 42.5 %collective-permute-start.42 = (bf16[2,192,768]{2,1,0:T(8,128)(2,1)S(1)}, bf16[2,192,768]{2,1,0:T(8,128)(2,1)}, u32[]{:S(2)}, u32[]{:S(2)}) collective-permute-start(bf16[2,192,768]{2,1,0:T(8,128)(2,1)S(1)} %slice_add_fusion.10), channel_id=1, source_target_pairs={{0,16},{4,20},{8,24},{12,28},{16,0},{20,4},{24,8},{28,12},{1,17},{... | collective-permute-start | bytes 1769480 | tf_op jit(solution)/shard_map/ppermute | solution.py:656
  373.0 32.0 %collective-permute-start.43 = (bf16[2,2,96,768]{3,2,0,1:T(8,128)(2,1)S(1)}, bf16[2,2,96,768]{3,2,0,1:T(8,128)(2,1)S(1)}, u32[]{:S(2)}, u32[]{:S(2)}) collective-permute-start(bf16[2,2,96,768]{3,2,0,1:T(8,128)(2,1)S(1)} %fusion.21), channel_id=1, source_target_pairs={{0,8},{4,12},{8,0},{12,4},{16,24},{20,28},{24,16},{28,20},{1,9},{5... | collective-permute-start | bytes 1769480 | tf_op jit(solution)/shard_map/ppermute | solution.py:656
  412.8 28.2 %collective-permute-start.47 = (bf16[2,192,768]{2,1,0:T(8,128)(2,1)S(1)}, bf16[2,192,768]{2,1,0:T(8,128)(2,1)S(1)}, u32[]{:S(2)}, u32[]{:S(2)}) collective-permute-start(bf16[2,192,768]{2,1,0:T(8,128)(2,1)S(1)} %slice_add_fusion.8), channel_id=1, source_target_pairs={{0,16},{4,20},{8,24},{12,28},{16,0},{20,4},{24,8},{28,12},{1,17},{... | collective-permute-start | bytes 1769480 | tf_op jit(solution)/shard_map/ppermute | solution.py:656
  416.1 37.2 %collective-permute-start.46 = (bf16[8,96,768]{2,1,0:T(8,128)(2,1)S(1)}, bf16[8,96,768]{2,1,0:T(8,128)(2,1)S(1)}, u32[]{:S(2)}, u32[]{:S(2)}) collective-permute-start(bf16[8,96,768]{2,1,0:T(8,128)(2,1)S(1)} %add.180), channel_id=1, source_target_pairs={{0,2},{1,3},{2,0},{3,1},{4,6},{5,7},{6,4},{7,5},{8,10},{9,11},{10,... | collective-permute-start | bytes 3538952 | tf_op jit(solution)/shard_map/ppermute | solution.py:656
  418.0 35.3 %collective-permute-start.48 = (bf16[608,768]{1,0:T(8,128)(2,1)S(1)}, bf16[608,768]{1,0:T(8,128)(2,1)S(1)}, u32[]{:S(2)}, u32[]{:S(2)}) collective-permute-start(bf16[608,768]{1,0:T(8,128)(2,1)S(1)} %bitcast_add_fusion.1), channel_id=1, source_target_pairs={{0,8},{4,12},{8,0},{12,4},{16,24},{20,28},{24,16},{28,20},{1,9},{5... | collective-permute-start | bytes 2801672 | tf_op jit(solution)/shard_map/ppermute | solution.py:656
  460.1 44.7 %all-to-all-start = ((bf16[8,112,768]{2,1,0:T(8,128)(2,1)}), bf16[8,112,768]{2,1,0:T(8,128)(2,1)S(1)}, u32[]{:S(2)}, u32[]{:S(2)}) async-start(bf16[8,112,768]{2,1,0:T(8,128)(2,1)} %fusion), calls=%async_computation | async-start | bytes 2752512 | tf_op jit(solution)/shard_map/all_to_all | solution.py:869
  468.2 32.0 %collective-permute-start.52 = (bf16[2,2,96,768]{3,2,0,1:T(8,128)(2,1)}, bf16[2,2,96,768]{3,2,0,1:T(8,128)(2,1)}, u32[]{:S(2)}, u32[]{:S(2)}) collective-permute-start(bf16[2,2,96,768]{3,2,0,1:T(8,128)(2,1)} %get-tuple-element.285), channel_id=1, source_target_pairs={{0,8},{4,12},{8,0},{12,4},{16,24},{20,28},{24,16},{28,20},{1,9},{5... | collective-permute-start | bytes 1769480 | tf_op jit(solution)/shard_map/ppermute | solution.py:656
  (73 other events, 723.9 us)
